TPU v7x, 256 devices: a whole 4x4x8 slice. The times are simulated.
256 devices in a mesh: lat: 16 (over y, x), grow: 16 (over z, core).
Axes of the slice: x: 4, y: 4, z: 8, core: 2. Of those that a mesh axis runs over, the one named last changes fastest.
Arguments:
- phase: float32 [256, 512, 512], P('grow', 'lat'), may hold values from -1 to 1
- solute: float32 [256, 512, 512], P('grow', 'lat'), may hold values from -1 to 0.5
- particle: float32 [256, 512, 512], P('grow', 'lat'), may hold values from 0 to 0.6
- inflow: float32 [8, 512, 512], P(None, 'lat'), may hold values from 0.1 to 0.5
Outputs:
- phase_out: float32 [256, 512, 512], P('grow', 'lat')
- solute_out: float32 [256, 512, 512], P('grow', 'lat')
- particle_out: float32 [256, 512, 512], P('grow', 'lat')
All inputs are finite; a program needn't handle non-finite values.
Results may differ from a plain program's by a relative error of at most 0.00002.
Values sent between devices are 32-bit elements; how exact they have to be, the bound alone decides.
No kernel may reach another device: no remote copies, remote signals or barrier semaphores. Data moves between devices by JAX's collectives and lax.ppermute only.
A program may use at most 64 MiB of HBM per device.

v0:
```python
import jax
import jax.numpy as jnp
from jax import lax
from jax.sharding import PartitionSpec as P

STEPS = 2
SHIFT = 8


time_step = 0.09
partition = 0.3
coupling = 2.0
beta_part = 1.0
solute_diff = 0.5
part_diff = 0.3
mobility = 0.5


def with_halo(cells, sides, width, closed):
    for axis, dim in sides:
        count = lax.axis_size(axis)
        ends = count if closed else count - 1
        head = lax.slice_in_dim(cells, 0, width, axis=dim)
        tail = lax.slice_in_dim(cells, cells.shape[dim] - width, cells.shape[dim], axis=dim)
        cells = jnp.concatenate(
            [
                lax.ppermute(tail, axis, [(i, (i + 1) % count) for i in range(ends)]),
                cells,
                lax.ppermute(head, axis, [((i + 1) % count, i) for i in range(ends)]),
            ],
            axis=dim,
        )
    return cells


def shifted(array, axis, by):
    peers = lax.axis_size(axis)
    pairs = [(i, i + by) for i in range(peers) if 0 <= i + by < peers]
    return lax.ppermute(array, axis, pairs)


def neighbours(field):
    centre = field[1:-1, 1:-1]
    return [
        field[2:, 1:-1],
        field[:-2, 1:-1],
        field[1:-1, 2:],
        field[1:-1, :-2],
        jnp.roll(centre, 1, axis=-1),
        jnp.roll(centre, -1, axis=-1),
    ]


def advance(grid, height, total):
    phi_all, sol_all, par_all = (grid[0], grid[1], grid[2])
    mobile = 0.5 * (1.0 - phi_all)
    carried = par_all * (1.0 - par_all)
    phi_c = phi_all[1:-1, 1:-1]
    sol_c = sol_all[1:-1, 1:-1]
    par_c = par_all[1:-1, 1:-1]
    mob_c = mobile[1:-1, 1:-1]
    car_c = carried[1:-1, 1:-1]
    phi_n = neighbours(phi_all)
    sol_n = neighbours(sol_all)
    par_n = neighbours(par_all)
    mob_n = neighbours(mobile)
    car_n = neighbours(carried)
    laplace = phi_n[0] + phi_n[1] + phi_n[2] + phi_n[3] + phi_n[4] + phi_n[5] - 6.0 * phi_c
    flux_sol = jnp.zeros_like(phi_c)
    flux_par = jnp.zeros_like(phi_c)
    drift = jnp.zeros_like(phi_c)
    for index in range(6):
        face_q = 0.5 * (mob_c + mob_n[index])
        flux_sol = flux_sol + face_q * (sol_n[index] - sol_c)
        flux_par = flux_par + face_q * (par_n[index] - par_c)
        drift = drift + 0.5 * (car_c + car_n[index]) * (phi_n[index] - phi_c)
    theta = (height - 0.5 * total) / total
    lag = 1.0 - (1.0 - partition) * theta
    well = (1.0 - phi_c * phi_c) * (1.0 - phi_c * phi_c)
    rate_phi = (
        laplace
        + phi_c
        - phi_c * phi_c * phi_c
        - coupling * well * (sol_c + theta + beta_part * par_c)
    ) / lag
    weight = 0.5 * (1.0 + partition) - 0.5 * (1.0 - partition) * phi_c
    rate_sol = (
        solute_diff * flux_sol + 0.5 * (1.0 + (1.0 - partition) * sol_c) * rate_phi
    ) / weight
    rate_par = part_diff * flux_par + mobility * drift
    return jnp.stack(
        [phi_c + time_step * rate_phi, sol_c + time_step * rate_sol, par_c + time_step * rate_par]
    )


def lateral(block):
    return with_halo(block, (("lat", 2),), 1, True)


def heights(first, count):
    return (first + jnp.arange(count, dtype=jnp.int32)).astype(jnp.float32)[:, None, None]


def on_device(phase, solute, particle, inflow):
    state = jnp.stack([phase, solute, particle])
    planes = phase.shape[0]
    grow_index = lax.axis_index("grow")
    is_top = grow_index == lax.axis_size("grow") - 1
    total = float(lax.axis_size("grow") * planes)
    for step in range(STEPS):
        grid = with_halo(state, (("grow", 1),), 1, False)
        lower = jnp.where(grow_index == 0, state[:, :1], grid[:, :1])
        upper = jnp.where(is_top, state[:, -1:], grid[:, -1:])
        grid = jnp.concatenate([lower, grid[:, 1:-1], upper], axis=1)
        grid = lateral(grid)
        state = advance(grid, heights(grow_index * planes, planes), total)
    moved = shifted(state[:, :SHIFT], "grow", -1)
    state = jnp.concatenate([state[:, SHIFT:], moved], axis=1)
    minus = jnp.full(inflow.shape, -1.0, dtype=jnp.float32)
    fill = jnp.stack([minus, minus, inflow])
    tail = jnp.where(is_top, fill, state[:, planes - SHIFT :])
    state = jnp.concatenate([state[:, : planes - SHIFT], tail], axis=1)
    return (state[0], state[1], state[2])


def solution(mesh):
    in_specs = (
        P("grow", "lat", None),
        P("grow", "lat", None),
        P("grow", "lat", None),
        P(None, "lat", None),
    )
    out_specs = (P("grow", "lat", None), P("grow", "lat", None), P("grow", "lat", None))
    return jax.shard_map(
        on_device, mesh=mesh, in_specs=in_specs, out_specs=out_specs, check_vma=False
    )
```

profile of v0, /device:TPU:127, one launch (start us, length us, event | category | flops | bytes accessed | tf_op | source)
XLA Modules:
  0.0 109.6 jit_solution(10376309985028899714)
XLA Ops:
  0.7 1.1 pad_maximum_fusion.11
  1.7 5.3 %collective-permute-start = (f32[3,1,32,512]{3,2,1,0:T(8,128)S(1)}, f32[3,1,32,512]{3,2,1,0:T(8,128)}, u32[]{:S(2)}, u32[]{:S(2)}) collective-permute-start(f32[3,1,32,512]{3,2,1,0:T(8,128)S(1)} %pad_maximum_fusion.11), channel_id=1, source_target_pairs={{0,1},{1,2},{2,3},{3,4},{4,5},{5,6},{6,7},{7,8},{8,9},{9,10},{10,1... | collective-permute-start | bytes 589832 | tf_op jit(solution)/shard_map/ppermute | solution.py:27
  7.1 2.6 %collective-permute-done = f32[3,1,32,512]{3,2,1,0:T(8,128)} collective-permute-done((f32[3,1,32,512]{3,2,1,0:T(8,128)S(1)}, f32[3,1,32,512]{3,2,1,0:T(8,128)}, u32[]{:S(2)}, u32[]{:S(2)}) %collective-permute-start) | collective-permute-done | bytes 196640 | tf_op jit(solution)/shard_map/ppermute | solution.py:27
  9.7 1.6 %broadcast_select_fusion.3 = (f32[3,1,32,512]{3,2,1,0:T(8,128)S(1)}, f32[3,1,32,512]{3,2,1,0:T(8,128)}) fusion(f32[3,1,32,512]{3,2,1,0:T(8,128)} %collective-permute-done, pred[]{:T(512)S(6)} %eq.7, f32[1,16,32,512]{3,2,1,0:T(8,128)S(1)} %bitcast.43, f32[1,16,32,512]{3,2,1,0:T(8,128)S(1)} %bitcast.47, f32[1,16,32,512]{3,2,1,0:T(8,128)S(1)} %bitcast.51), kind=kLoop, calls=%fused_computation.223 | loop fusion | flops 147456 | bytes 3735553 | tf_op jit(solution)/shard_map/jit(_where)/select_n | solution.py:112
  11.3 1.9 %collective-permute-start.1 = (f32[3,1,32,512]{3,2,1,0:T(8,128)}, f32[3,1,32,512]{3,2,1,0:T(8,128)}, u32[]{:S(2)}, u32[]{:S(2)}) collective-permute-start(f32[3,1,32,512]{3,2,1,0:T(8,128)} %get-tuple-element.10), channel_id=1, source_target_pairs={{1,0},{2,1},{3,2},{4,3},{5,4},{6,5},{7,6},{8,7},{9,8},{10,9},{11,1... | collective-permute-start | bytes 589832 | tf_op jit(solution)/shard_map/ppermute | solution.py:29
  13.2 7.4 %collective-permute-done.1 = f32[3,1,32,512]{3,2,1,0:T(8,128)} collective-permute-done((f32[3,1,32,512]{3,2,1,0:T(8,128)}, f32[3,1,32,512]{3,2,1,0:T(8,128)}, u32[]{:S(2)}, u32[]{:S(2)}) %collective-permute-start.1) | collective-permute-done | bytes 196640 | tf_op jit(solution)/shard_map/ppermute | solution.py:29
  20.7 1.0 broadcast_select_fusion.1
  21.6 0.2 pad_maximum_fusion.23
  21.9 1.5 %collective-permute-start.3 = (f32[3,18,1,512]{3,2,1,0:T(1,128)S(1)}, f32[3,18,1,512]{3,2,1,0:T(1,128)S(1)}, u32[]{:S(2)}, u32[]{:S(2)}) collective-permute-start(f32[3,18,1,512]{3,2,1,0:T(1,128)S(1)} %get-tuple-element.24), channel_id=1, source_target_pairs={{16,0},{32,16},{48,32},{64,48},{80,64},{96,80},{112,96},{128,112},... | collective-permute-start | bytes 331784 | tf_op jit(solution)/shard_map/ppermute | solution.py:29
  23.4 2.2 %collective-permute-done.2 = f32[3,18,1,512]{3,2,1,0:T(1,128)S(1)} collective-permute-done((f32[3,18,1,512]{3,2,1,0:T(1,128)S(1)}, f32[3,18,1,512]{3,2,1,0:T(1,128)S(1)}, u32[]{:S(2)}, u32[]{:S(2)}) %collective-permute-start.2) | collective-permute-done | bytes 110624 | tf_op jit(solution)/shard_map/ppermute | solution.py:27
  25.6 3.3 %collective-permute-done.3 = f32[3,18,1,512]{3,2,1,0:T(1,128)S(1)} collective-permute-done((f32[3,18,1,512]{3,2,1,0:T(1,128)S(1)}, f32[3,18,1,512]{3,2,1,0:T(1,128)S(1)}, u32[]{:S(2)}, u32[]{:S(2)}) %collective-permute-start.3) | collective-permute-done | bytes 110624 | tf_op jit(solution)/shard_map/ppermute | solution.py:29
  28.9 1.0 pad_maximum_fusion
  29.9 0.5 slice_bitcast_fusion.4
  30.4 1.0 fusion.140
  31.4 0.2 fusion.139
  31.7 0.4 subtract_multiply_fusion.3
  32.0 1.1 fusion.142
  33.1 0.9 fusion.141
  34.1 0.5 fusion.147
  34.7 1.4 %add_bitcast_fusion.3 = (f32[1,16,32,512]{3,2,1,0:T(8,128)S(1)}, f32[16,32,512]{2,1,0:T(8,128)S(1)}) fusion(f32[18,34,512]{2,1,0:T(8,128)S(1)} %get-tuple-element.18, f32[16]{0:T(128)S(1)} %get-tuple-element.78, f32[18,34,512]{2,1,0:T(8,128)S(1)} %get-tuple-element.17, f32[16]{0:T(128)S(1)} %get-tuple-element.79, f32[18,34,512]{2,1,0:T(8,128)S(1)} %get-tuple-element.16, ...), kind=kLoop, calls=%fused_computation.203 | loop fusion | flops 6029312 | bytes 11534464 | tf_op jit(solution)/shard_map/stack | solution.py:91
  36.1 3.0 %add_bitcast_fusion.2 = f32[1,16,32,512]{3,2,1,0:T(8,128)S(1)} fusion(f32[16,32,1]{2,1,0:T(8,128)S(1)} %get-tuple-element.51, f32[16,32,511]{2,1,0:T(8,128)S(1)} %get-tuple-element.53, f32[16,32,511]{2,1,0:T(8,128)S(1)} %get-tuple-element.52, f32[16,32,1]{2,1,0:T(8,128)S(1)} %get-tuple-element.50, f32[18,34,512]{2,1,0:T(8,128)S(1)} %get-tuple-element.16, ...), kind=kLoop, calls=%fused_computation.202 | loop fusion | flops 11534336 | bytes 17825792 | tf_op jit(solution)/shard_map/stack | solution.py:91
  39.1 6.1 %fusion.70 = f32[1,16,32,512]{3,2,1,0:T(8,128)S(1)} fusion(f32[18,34,512]{2,1,0:T(8,128)S(1)} %get-tuple-element.20, f32[18,34,512]{2,1,0:T(8,128)S(1)} %get-tuple-element.17, f32[16,32,511]{2,1,0:T(8,128)S(1)} %get-tuple-element.67, f32[16,32,1]{2,1,0:T(8,128)S(1)} %get-tuple-element.69, f32[16,32,1]{2,1,0:T(8,128)S(1)} %get-tuple-element.68, ...), kind=kLoop, calls=%fused_computation.110 | loop fusion | flops 18612224 | bytes 30408704 | tf_op jit(solution)/shard_map/stack | solution.py:91
  45.3 3.2 %collective-permute-start.4 = (f32[3,1,32,512]{3,2,1,0:T(8,128)S(1)}, f32[3,1,32,512]{3,2,1,0:T(8,128)S(1)}, u32[]{:S(2)}, u32[]{:S(2)}) collective-permute-start(f32[3,1,32,512]{3,2,1,0:T(8,128)S(1)} %pad_maximum_fusion.8), channel_id=1, source_target_pairs={{0,1},{1,2},{2,3},{3,4},{4,5},{5,6},{6,7},{7,8},{8,9},{9,10},{10,1... | collective-permute-start | bytes 589832 | tf_op jit(solution)/shard_map/ppermute | solution.py:27
  48.5 2.6 %collective-permute-done.4 = f32[3,1,32,512]{3,2,1,0:T(8,128)S(1)} collective-permute-done((f32[3,1,32,512]{3,2,1,0:T(8,128)S(1)}, f32[3,1,32,512]{3,2,1,0:T(8,128)S(1)}, u32[]{:S(2)}, u32[]{:S(2)}) %collective-permute-start.4) | collective-permute-done | bytes 196640 | tf_op jit(solution)/shard_map/ppermute | solution.py:27
  51.1 1.9 %collective-permute-start.5 = (f32[3,1,32,512]{3,2,1,0:T(8,128)S(1)}, f32[3,1,32,512]{3,2,1,0:T(8,128)S(1)}, u32[]{:S(2)}, u32[]{:S(2)}) collective-permute-start(f32[3,1,32,512]{3,2,1,0:T(8,128)S(1)} %get-tuple-element.6), channel_id=1, source_target_pairs={{1,0},{2,1},{3,2},{4,3},{5,4},{6,5},{7,6},{8,7},{9,8},{10,9},{11,1... | collective-permute-start | bytes 589832 | tf_op jit(solution)/shard_map/ppermute | solution.py:29
  53.0 7.0 %collective-permute-done.5 = f32[3,1,32,512]{3,2,1,0:T(8,128)S(1)} collective-permute-done((f32[3,1,32,512]{3,2,1,0:T(8,128)S(1)}, f32[3,1,32,512]{3,2,1,0:T(8,128)S(1)}, u32[]{:S(2)}, u32[]{:S(2)}) %collective-permute-start.5) | collective-permute-done | bytes 196640 | tf_op jit(solution)/shard_map/ppermute | solution.py:29
  60.1 0.2 pad_maximum_fusion.18
  60.4 1.5 %collective-permute-start.7 = (f32[3,18,1,512]{3,2,1,0:T(1,128)S(1)}, f32[3,18,1,512]{3,2,1,0:T(1,128)S(1)}, u32[]{:S(2)}, u32[]{:S(2)}) collective-permute-start(f32[3,18,1,512]{3,2,1,0:T(1,128)S(1)} %get-tuple-element.22), channel_id=1, source_target_pairs={{16,0},{32,16},{48,32},{64,48},{80,64},{96,80},{112,96},{128,112},... | collective-permute-start | bytes 331784 | tf_op jit(solution)/shard_map/ppermute | solution.py:29
  61.8 2.1 %collective-permute-done.6 = f32[3,18,1,512]{3,2,1,0:T(1,128)S(1)} collective-permute-done((f32[3,18,1,512]{3,2,1,0:T(1,128)S(1)}, f32[3,18,1,512]{3,2,1,0:T(1,128)S(1)}, u32[]{:S(2)}, u32[]{:S(2)}) %collective-permute-start.6) | collective-permute-done | bytes 110624 | tf_op jit(solution)/shard_map/ppermute | solution.py:27
  64.0 3.6 %collective-permute-done.7 = f32[3,18,1,512]{3,2,1,0:T(1,128)S(1)} collective-permute-done((f32[3,18,1,512]{3,2,1,0:T(1,128)S(1)}, f32[3,18,1,512]{3,2,1,0:T(1,128)S(1)}, u32[]{:S(2)}, u32[]{:S(2)}) %collective-permute-start.7) | collective-permute-done | bytes 110624 | tf_op jit(solution)/shard_map/ppermute | solution.py:29
  67.6 1.0 pad_maximum_fusion.1
  68.6 0.5 slice_bitcast_fusion.1
  69.1 0.5 fusion.134
  69.7 0.4 subtract_multiply_fusion.2
  70.1 0.5 fusion.130
  70.8 0.5 fusion.132
  71.4 0.5 fusion.137
  72.0 0.5 fusion.135
  72.5 0.8 fusion.136
  73.3 1.4 %add_bitcast_fusion.1 = (f32[1,16,32,512]{3,2,1,0:T(8,128)S(1)}, f32[16,32,512]{2,1,0:T(8,128)S(1)}) fusion(f32[18,34,512]{2,1,0:T(8,128)S(1)} %get-tuple-element.13, f32[16]{0:T(128)S(1)} %get-tuple-element.78, f32[18,34,512]{2,1,0:T(8,128)S(1)} %get-tuple-element.12, f32[16]{0:T(128)S(1)} %get-tuple-element.79, f32[18,34,512]{2,1,0:T(8,128)S(1)} %get-tuple-element.11, ...), kind=kLoop, calls=%fused_computation.201 | loop fusion | flops 6029312 | bytes 11534464 | tf_op jit(solution)/shard_map/stack | solution.py:91
  74.8 3.0 %add_bitcast_fusion = f32[1,16,32,512]{3,2,1,0:T(8,128)S(1)} fusion(f32[16,32,1]{2,1,0:T(8,128)S(1)} %get-tuple-element.31, f32[16,32,511]{2,1,0:T(8,128)S(1)} %get-tuple-element.33, f32[16,32,511]{2,1,0:T(8,128)S(1)} %get-tuple-element.32, f32[16,32,1]{2,1,0:T(8,128)S(1)} %get-tuple-element.30, f32[18,34,512]{2,1,0:T(8,128)S(1)} %get-tuple-element.11, ...), kind=kLoop, calls=%fused_computation.200 | loop fusion | flops 11534336 | bytes 17825792 | tf_op jit(solution)/shard_map/stack | solution.py:91
  77.8 6.1 %fusion.26 = f32[1,16,32,512]{3,2,1,0:T(8,128)S(1)} fusion(f32[18,34,512]{2,1,0:T(8,128)S(1)} %get-tuple-element.15, f32[18,34,512]{2,1,0:T(8,128)S(1)} %get-tuple-element.12, f32[16,32,511]{2,1,0:T(8,128)S(1)} %get-tuple-element.47, f32[16,32,1]{2,1,0:T(8,128)S(1)} %get-tuple-element.49, f32[16,32,1]{2,1,0:T(8,128)S(1)} %get-tuple-element.48, ...), kind=kLoop, calls=%fused_computation.50 | loop fusion | flops 18612224 | bytes 30408704 | tf_op jit(solution)/shard_map/stack | solution.py:91
  83.9 0.3 pad_maximum_fusion.2
  84.3 0.4 fusion.128
  84.7 1.9 %collective-permute-start.8 = (f32[3,8,32,512]{3,2,1,0:T(8,128)S(1)}, f32[3,8,32,512]{3,2,1,0:T(8,128)S(1)}, u32[]{:S(2)}, u32[]{:S(2)}) collective-permute-start(f32[3,8,32,512]{3,2,1,0:T(8,128)S(1)} %get-tuple-element.28), channel_id=1, source_target_pairs={{1,0},{2,1},{3,2},{4,3},{5,4},{6,5},{7,6},{8,7},{9,8},{10,9},{11,1... | collective-permute-start | bytes 4718600 | tf_op jit(solution)/shard_map/ppermute | solution.py:39
  86.6 21.0 %collective-permute-done.8 = f32[3,8,32,512]{3,2,1,0:T(8,128)S(1)} collective-permute-done((f32[3,8,32,512]{3,2,1,0:T(8,128)S(1)}, f32[3,8,32,512]{3,2,1,0:T(8,128)S(1)}, u32[]{:S(2)}, u32[]{:S(2)}) %collective-permute-start.8) | collective-permute-done | bytes 1572896 | tf_op jit(solution)/shard_map/ppermute | solution.py:39
  107.6 0.2 pad_select_fusion
  107.9 1.8 %fusion.16 = (f32[16,32,512]{2,1,0:T(8,128)}, f32[16,32,512]{2,1,0:T(8,128)}, f32[16,32,512]{2,1,0:T(8,128)}) fusion(f32[3,8,32,512]{3,2,1,0:T(8,128)S(1)} %pad_select_fusion, f32[3,8,32,512]{3,2,1,0:T(8,128)S(1)} %get-tuple-element.29), kind=kLoop, calls=%fused_computation.39 | loop fusion | flops 786432 | bytes 6291456 | tf_op jit(solution)/shard_map/squeeze | solution.py:123
  (19 shorter events, 1.0 us)
Async XLA Ops:
  0.6 9.0 %copy-start = (f32[16,32,512]{2,1,0:T(8,128)S(1)}, f32[16,32,512]{2,1,0:T(8,128)}, u32[]{:S(2)}) copy-start(f32[16,32,512]{2,1,0:T(8,128)} %param.6) | copy-start | bytes 3145732
  0.6 9.0 %copy-start.1 = (f32[16,32,512]{2,1,0:T(8,128)S(1)}, f32[16,32,512]{2,1,0:T(8,128)}, u32[]{:S(2)}) copy-start(f32[16,32,512]{2,1,0:T(8,128)} %param.5) | copy-start | bytes 3145732
  0.7 9.0 %copy-start.2 = (f32[16,32,512]{2,1,0:T(8,128)S(1)}, f32[16,32,512]{2,1,0:T(8,128)}, u32[]{:S(2)}) copy-start(f32[16,32,512]{2,1,0:T(8,128)} %param.4) | copy-start | bytes 3145732
  1.7 7.9 %collective-permute-start = (f32[3,1,32,512]{3,2,1,0:T(8,128)S(1)}, f32[3,1,32,512]{3,2,1,0:T(8,128)}, u32[]{:S(2)}, u32[]{:S(2)}) collective-permute-start(f32[3,1,32,512]{3,2,1,0:T(8,128)S(1)} %pad_maximum_fusion.11), channel_id=1, source_target_pairs={{0,1},{1,2},{2,3},{3,4},{4,5},{5,6},{6,7},{7,8},{8,9},{9,10},{10,1... | collective-permute-start | bytes 589832 | tf_op jit(solution)/shard_map/ppermute | solution.py:27
  11.3 9.4 %collective-permute-start.1 = (f32[3,1,32,512]{3,2,1,0:T(8,128)}, f32[3,1,32,512]{3,2,1,0:T(8,128)}, u32[]{:S(2)}, u32[]{:S(2)}) collective-permute-start(f32[3,1,32,512]{3,2,1,0:T(8,128)} %get-tuple-element.10), channel_id=1, source_target_pairs={{1,0},{2,1},{3,2},{4,3},{5,4},{6,5},{7,6},{8,7},{9,8},{10,9},{11,1... | collective-permute-start | bytes 589832 | tf_op jit(solution)/shard_map/ppermute | solution.py:29
  21.8 3.8 %collective-permute-start.2 = (f32[3,18,1,512]{3,2,1,0:T(1,128)S(1)}, f32[3,18,1,512]{3,2,1,0:T(1,128)S(1)}, u32[]{:S(2)}, u32[]{:S(2)}) collective-permute-start(f32[3,18,1,512]{3,2,1,0:T(1,128)S(1)} %get-tuple-element.23), channel_id=1, source_target_pairs={{0,16},{16,32},{32,48},{48,64},{64,80},{80,96},{96,112},{112,128},... | collective-permute-start | bytes 331784 | tf_op jit(solution)/shard_map/ppermute | solution.py:27
  21.9 7.0 %collective-permute-start.3 = (f32[3,18,1,512]{3,2,1,0:T(1,128)S(1)}, f32[3,18,1,512]{3,2,1,0:T(1,128)S(1)}, u32[]{:S(2)}, u32[]{:S(2)}) collective-permute-start(f32[3,18,1,512]{3,2,1,0:T(1,128)S(1)} %get-tuple-element.24), channel_id=1, source_target_pairs={{16,0},{32,16},{48,32},{64,48},{80,64},{96,80},{112,96},{128,112},... | collective-permute-start | bytes 331784 | tf_op jit(solution)/shard_map/ppermute | solution.py:29
  45.3 5.8 %collective-permute-start.4 = (f32[3,1,32,512]{3,2,1,0:T(8,128)S(1)}, f32[3,1,32,512]{3,2,1,0:T(8,128)S(1)}, u32[]{:S(2)}, u32[]{:S(2)}) collective-permute-start(f32[3,1,32,512]{3,2,1,0:T(8,128)S(1)} %pad_maximum_fusion.8), channel_id=1, source_target_pairs={{0,1},{1,2},{2,3},{3,4},{4,5},{5,6},{6,7},{7,8},{8,9},{9,10},{10,1... | collective-permute-start | bytes 589832 | tf_op jit(solution)/shard_map/ppermute | solution.py:27
  51.1 8.9 %collective-permute-start.5 = (f32[3,1,32,512]{3,2,1,0:T(8,128)S(1)}, f32[3,1,32,512]{3,2,1,0:T(8,128)S(1)}, u32[]{:S(2)}, u32[]{:S(2)}) collective-permute-start(f32[3,1,32,512]{3,2,1,0:T(8,128)S(1)} %get-tuple-element.6), channel_id=1, source_target_pairs={{1,0},{2,1},{3,2},{4,3},{5,4},{6,5},{7,6},{8,7},{9,8},{10,9},{11,1... | collective-permute-start | bytes 589832 | tf_op jit(solution)/shard_map/ppermute | solution.py:29
  60.3 3.7 %collective-permute-start.6 = (f32[3,18,1,512]{3,2,1,0:T(1,128)S(1)}, f32[3,18,1,512]{3,2,1,0:T(1,128)S(1)}, u32[]{:S(2)}, u32[]{:S(2)}) collective-permute-start(f32[3,18,1,512]{3,2,1,0:T(1,128)S(1)} %get-tuple-element.21), channel_id=1, source_target_pairs={{0,16},{16,32},{32,48},{48,64},{64,80},{80,96},{96,112},{112,128},... | collective-permute-start | bytes 331784 | tf_op jit(solution)/shard_map/ppermute | solution.py:27
  60.4 7.2 %collective-permute-start.7 = (f32[3,18,1,512]{3,2,1,0:T(1,128)S(1)}, f32[3,18,1,512]{3,2,1,0:T(1,128)S(1)}, u32[]{:S(2)}, u32[]{:S(2)}) collective-permute-start(f32[3,18,1,512]{3,2,1,0:T(1,128)S(1)} %get-tuple-element.22), channel_id=1, source_target_pairs={{16,0},{32,16},{48,32},{64,48},{80,64},{96,80},{112,96},{128,112},... | collective-permute-start | bytes 331784 | tf_op jit(solution)/shard_map/ppermute | solution.py:29
  84.2 23.4 %copy-start.3 = (f32[8,32,512]{2,1,0:T(8,128)S(1)}, f32[8,32,512]{2,1,0:T(8,128)}, u32[]{:S(2)}) copy-start(f32[8,32,512]{2,1,0:T(8,128)} %param.7) | copy-start | bytes 1572868
  84.7 22.9 %collective-permute-start.8 = (f32[3,8,32,512]{3,2,1,0:T(8,128)S(1)}, f32[3,8,32,512]{3,2,1,0:T(8,128)S(1)}, u32[]{:S(2)}, u32[]{:S(2)}) collective-permute-start(f32[3,8,32,512]{3,2,1,0:T(8,128)S(1)} %get-tuple-element.28), channel_id=1, source_target_pairs={{1,0},{2,1},{3,2},{4,3},{5,4},{6,5},{7,6},{8,7},{9,8},{10,9},{11,1... | collective-permute-start | bytes 4718600 | tf_op jit(solution)/shard_map/ppermute | solution.py:39
where the time goes:
time: 110 us
  waiting for transfers between devices  51.9 us (47%)
  other arithmetic  30.3 us (28%)
  starting transfers between devices  17.3 us (16%)
  local copies, waits for them, and re-layouts  9.05 us (8%)
    another operation x8, other arithmetic, advance(): jnp.stack([phi_c + time_step * rate_phi, sol_c + time_step * rate_sol, pa...  21.4 us
    ppermute x4, waiting for transfers between devices, with_halo(): lax.ppermute(head, axis, [((i + 1) % count, i) for i in range(ends)])  21.4 us
    ppermute x1, waiting for transfers between devices, shifted(): return lax.ppermute(array, axis, pairs)  21 us
    ppermute x4, waiting for transfers between devices, with_halo(): lax.ppermute(tail, axis, [(i, (i + 1) % count) for i in range(ends)])  9.54 us
    ppermute x4, starting transfers between devices, with_halo(): lax.ppermute(tail, axis, [(i, (i + 1) % count) for i in range(ends)])  8.68 us
    ppermute x4, starting transfers between devices, with_halo(): lax.ppermute(head, axis, [((i + 1) % count, i) for i in range(ends)])  6.74 us
    slice x10, local copies, waits for them, and re-layouts, neighbours(): jnp.roll(centre, 1, axis=-1)  5.11 us
    slice x6, local copies, waits for them, and re-layouts, neighbours(): jnp.roll(centre, -1, axis=-1)  2.53 us
  transfers between devices with their start and end apart: 9, of which 9 were waited for; matrix products, arithmetic and copies ran while one was open for 0% of the time, Pallas kernels for 0%

commit v1 on v0

v1 whole, which is shorter than its diff:
```python
import functools

import jax
import jax.numpy as jnp
from jax import lax
from jax.experimental import pallas as pl
from jax.experimental.pallas import tpu as pltpu
from jax.sharding import PartitionSpec as P

STEPS = 2
SHIFT = 8

DT = 0.09
PART = 0.3
DU = 0.5
DP = 0.3
MOB = 0.5
ALPHA = DT * DP / 4.0
MU = DT * MOB / 2.0

HALO = STEPS
ROWS = 32
EXT = ROWS + 8
TILES = EXT // 8
FAR = SHIFT + HALO


def tile(t):
    return pl.ds(8 * t, 8)


def extend(base, i, t, s, u, p):
    scaled = ALPHA * p
    carried = p * (MU - MU * p)
    base[i, 3, tile(t)] = scaled + carried
    base[i, 4, tile(t)] = s * (scaled - carried)
    base[i, 5, tile(t)] = s * u


def put(base, i, t, s, u, p):
    base[i, 0, tile(t)] = s
    base[i, 1, tile(t)] = u
    base[i, 2, tile(t)] = p
    extend(base, i, t, s, u, p)


def around(base, i, f, t, sub):
    c = base[i, f, tile(t)]
    before = base[i, f, tile((t - 1) % TILES)]
    after = base[i, f, tile((t + 1) % TILES)]
    n = base[i - 1, f, tile(t)] + base[i + 1, f, tile(t)]
    n = n + pltpu.roll(jnp.where(sub == 7, before, c), 1, 0)
    n = n + pltpu.roll(jnp.where(sub == 0, after, c), 7, 0)
    n = n + pltpu.roll(c, 1, 1)
    n = n + pltpu.roll(c, c.shape[1] - 1, 1)
    return c, n


def advance(base, i, t, sub, theta, gain):
    s, ns = around(base, i, 0, t, sub)
    u, nu = around(base, i, 1, t, sub)
    p = base[i, 2, tile(t)]
    g, ng = around(base, i, 3, t, sub)
    sh, nsh = around(base, i, 4, t, sub)
    su, nsu = around(base, i, 5, t, sub)
    phi = 1.0 - s
    hump = 1.0 - phi * phi
    drive = (u + p) + theta
    rise = ((6.0 * s - ns) + hump * (phi - (hump * drive) * 2.0)) * gain
    flux = (s * nu + nsu) - (u * ns + 6.0 * su)
    weight = PART + (0.5 * (1.0 - PART)) * s
    source = (DT * DU / 4.0) * flux + (0.5 + (0.5 * (1.0 - PART)) * u) * rise
    u_new = u + source * pltpu.reciprocal(weight, full_range=False)
    p_new = p + ((s * ng + nsh) - (g * ns + 6.0 * sh))
    return phi + rise, u_new, p_new


def segment(own, last, start, n_new, total, planes, *refs):
    refs = list(refs)
    take = lambda n: [refs.pop(0) for _ in range(n)]
    if own:
        fields = take(3)
    else:
        (far,) = take(1)
    left, right = take(2)
    if not own:
        (kept, inflow), _ = take(2), take(3)
    outs = take(3)
    if not last:
        (keep,) = take(1)
    raw, sides, base0, base1, res, in_sem, out_sem, keep_sem = take(8)
    old = 0 if own else 2
    n_in = n_new + old
    n_mid = n_in - 2 if own else n_new + 2
    n_out = n_mid - 2
    mid = start + 1 if own else start - 1
    out0 = mid + 1
    if not own:
        fill, kept_vmem = take(2)
    grow = lax.axis_index("grow")
    is_top = grow == lax.axis_size("grow") - 1
    sub = lax.broadcasted_iota(jnp.int32, (8, raw.shape[-1]), 0)

    copies = []
    if not own:
        k = pltpu.make_async_copy(kept, kept_vmem, keep_sem.at[0])
        k.start()
    for f in range(3):
        src = fields[f].at[pl.ds(start, n_new)] if own else far.at[f]
        copies.append(pltpu.make_async_copy(src, raw.at[f], in_sem.at[f]))
    copies.append(pltpu.make_async_copy(left, sides.at[0], in_sem.at[3]))
    copies.append(pltpu.make_async_copy(right, sides.at[1], in_sem.at[4]))
    for c in copies:
        c.start()
    if not own:
        first_fill = max(0, planes - out0)
        n_fill = n_out - first_fill
        f = pltpu.make_async_copy(
            inflow.at[pl.ds(out0 + first_fill - planes, n_fill)], fill.at[pl.ds(first_fill, n_fill)], in_sem.at[5]
        )
        f.start()
        k.wait()

        def revive(i, _):
            for which, base in ((0, base0), (1, base1)):
                for t in range(TILES):
                    s, u, p = (kept_vmem[which, i, f, tile(t)] for f in range(3))
                    put(base, i, t, s, u, p)
            return 0

        lax.fori_loop(0, 2, revive, 0)
    for c in copies:
        c.wait()

    def load(i, _):
        for t in range(ROWS // 8):
            phi, u, p = (raw[f, i, tile(t)] for f in range(3))
            put(base0, i + old, t, 1.0 - phi, u, p)
        edge = []
        for f in range(3):
            low, high = sides[0, f, i], sides[1, f, i]
            edge.append(jnp.concatenate([high, jnp.zeros((4, high.shape[1]), jnp.float32), low], axis=0))
        put(base0, i + old, TILES - 1, 1.0 - edge[0], edge[1], edge[2])
        return 0

    lax.fori_loop(0, n_new, load, 0)

    above = planes - start
    if not own and 0 <= above < n_in:

        @pl.when(is_top)
        def _():
            base0[above] = base0[above - 1]

    def coefficients(plane):
        height = (grow * planes + plane).astype(jnp.float32)
        theta = (height - 0.5 * total) / total
        lag = jnp.full(sub.shape, 1.0 - (1.0 - PART) * theta, jnp.float32)
        return theta, DT / lag

    def middle(i, _):
        at = i + 1 if own else i - 1
        theta, gain = coefficients(mid + i)
        for t in range(TILES):
            phi, u, p = advance(base0, at, t, sub, theta, gain)
            put(base1, i, t, 1.0 - phi, u, p)
        return 0

    lax.fori_loop(0 if own else 2, n_mid, middle, 0)

    above = planes - mid
    if not own and 0 <= above < n_mid:

        @pl.when(is_top)
        def _():
            base1[above] = base1[above - 1]

    keeping = []
    if not last:
        for which, base, n in ((0, base0, n_in), (1, base1, n_mid)):
            keeping.append(
                pltpu.make_async_copy(base.at[pl.ds(n - 2, 2), pl.ds(0, 3)], keep.at[which], keep_sem.at[1 + which])
            )
        for c in keeping:
            c.start()

    def write(i):
        return [
            pltpu.make_async_copy(res.at[f, i], outs[f].at[out0 - SHIFT + i], out_sem.at[f, i]) for f in range(3)
        ]

    if not own:
        f.wait()

    def final(i, _):
        theta, gain = coefficients(out0 + i)
        for t in range(ROWS // 8):
            phi, u, p = advance(base1, i + 1, t, sub, theta, gain)
            res[0, i, tile(t)] = phi
            res[1, i, tile(t)] = u
            res[2, i, tile(t)] = p
        if not own:

            @pl.when(jnp.logical_and(is_top, out0 + i >= planes))
            def _():
                res[0, i] = jnp.full(res.shape[2:], -1.0, jnp.float32)
                res[1, i] = jnp.full(res.shape[2:], -1.0, jnp.float32)
                res[2, i] = fill[i]

        for c in write(i):
            c.start()
        return 0

    lax.fori_loop(0, n_out, final, 0)

    def finish(i, _):
        for c in write(i):
            c.wait()
        return 0

    lax.fori_loop(0, n_out, finish, 0)
    for c in keeping:
        c.wait()


def run(own, last, start, n_new, total, planes, shape, ins, outs=None):
    ny = shape[2]
    old = 0 if own else 2
    n_in = n_new + old
    n_mid = n_in - 2 if own else n_new + 2
    n_out = n_mid - 2
    any_ = pl.BlockSpec(memory_space=pl.ANY)
    f32 = jnp.float32
    out_shape = [jax.ShapeDtypeStruct(shape, f32)] * 3
    if not last:
        out_shape.append(jax.ShapeDtypeStruct((2, 2, 3, EXT, ny), f32))
    scratch = [
        pltpu.VMEM((3, n_new, ROWS, ny), f32),
        pltpu.VMEM((2, 3, n_new, HALO, ny), f32),
        pltpu.VMEM((n_in, 6, EXT, ny), f32),
        pltpu.VMEM((n_mid, 6, EXT, ny), f32),
        pltpu.VMEM((3, n_out, ROWS, ny), f32),
        pltpu.SemaphoreType.DMA((6,)),
        pltpu.SemaphoreType.DMA((3, n_out)),
        pltpu.SemaphoreType.DMA((3,)),
    ]
    if not own:
        scratch += [pltpu.VMEM((n_out, ROWS, ny), f32), pltpu.VMEM((2, 2, 3, EXT, ny), f32)]
    args = list(ins) + (list(outs) if outs is not None else [])
    alias = {} if outs is None else {len(ins) + k: k for k in range(3)}
    cells = (n_in * EXT + n_mid * EXT + n_out * ROWS) * ny
    return pl.pallas_call(
        functools.partial(segment, own, last, start, n_new, total, planes),
        out_shape=out_shape,
        in_specs=[any_] * len(args),
        out_specs=[any_] * len(out_shape),
        scratch_shapes=scratch,
        input_output_aliases=alias,
        compiler_params=pltpu.CompilerParams(vmem_limit_bytes=28 << 20),
        cost_estimate=pl.CostEstimate(flops=60 * cells, bytes_accessed=20 * cells, transcendentals=0),
        name="first_run" if own else "last_run" if last else "next_run",
    )(*args)


NEAR = 7


def on_device(phase, solute, particle, inflow):
    planes, rows, ny = phase.shape
    n_lat, n_grow = lax.axis_size("lat"), lax.axis_size("grow")
    total = float(n_grow * planes)
    down = [(i + 1, i) for i in range(n_grow - 1)]
    east = [(i, (i + 1) % n_lat) for i in range(n_lat)]
    west = [((i + 1) % n_lat, i) for i in range(n_lat)]
    fields = (phase, solute, particle)

    def cut(lo, hi, a, b):
        return jnp.stack([f[lo:hi, a:b] for f in fields])

    def diagonal(pairs):
        return [(l * n_grow + g, m * n_grow + h) for l, m in pairs for g, h in down]

    both = ("lat", "grow")
    near = lax.ppermute(cut(0, NEAR, 0, rows), "grow", down)
    lo = planes - SHIFT - HALO
    left = lax.ppermute(cut(lo, planes, rows - HALO, rows), "lat", east)
    right = lax.ppermute(cut(lo, planes, 0, HALO), "lat", west)
    far_left = lax.ppermute(cut(0, FAR, rows - HALO, rows), both, diagonal(east))
    far_right = lax.ppermute(cut(0, FAR, 0, HALO), both, diagonal(west))
    rest = lax.ppermute(cut(NEAR, FAR, 0, rows), "grow", down)

    *outs, keep = run(True, False, lo, planes - lo, total, planes, phase.shape, (*fields, left, right))
    *outs, keep = run(
        False, False, planes - 2, NEAR, total, planes, phase.shape,
        (near, far_left[:, :NEAR], far_right[:, :NEAR], keep, inflow), outs,
    )
    return tuple(
        run(
            False, True, planes - 2 + NEAR, FAR - NEAR, total, planes, phase.shape,
            (rest, far_left[:, NEAR:], far_right[:, NEAR:], keep, inflow), outs,
        )
    )


def solution(mesh):
    in_specs = (
        P("grow", "lat", None),
        P("grow", "lat", None),
        P("grow", "lat", None),
        P(None, "lat", None),
    )
    out_specs = (P("grow", "lat", None), P("grow", "lat", None), P("grow", "lat", None))
    return jax.shard_map(
        on_device, mesh=mesh, in_specs=in_specs, out_specs=out_specs, check_vma=False
    )
```

time: 110 us -> 59.2 us (0.54)
  the two profiles are of different devices: /device:TPU:127 before, /device:TPU:1 now
where the time goes in v1:
time: 59.2 us; the launch traced here: 58.6 us
  waiting for transfers between devices  21.5 us (36%)
  Pallas kernels  18.4 us (31%)
  starting transfers between devices  14.9 us (25%)
  local copies, waits for them, and re-layouts  2.55 us (4%)
  between operations  0.89 us (2%)
    pallas_call x3, Pallas kernels, run(): pl.pallas_call(functools.partial(segment, own, last, start, n_new, total,...  18.4 us
    ppermute x1, waiting for transfers between devices, on_device(): lax.ppermute(cut(0, FAR, rows - HALO, rows), both, diagonal(east))  18.3 us
    ppermute x1, starting transfers between devices, on_device(): near = lax.ppermute(cut(0, NEAR, 0, rows), 'grow', down)  5.28 us
    ppermute x1, starting transfers between devices, on_device(): far_right = lax.ppermute(cut(0, FAR, 0, HALO), both, diagonal(west))  5.15 us
    ppermute x1, waiting for transfers between devices, on_device(): right = lax.ppermute(cut(lo, planes, 0, HALO), 'lat', west)  3.11 us
    another operation x6, local copies, waits for them, and re-layouts, cut(): return jnp.stack([f[lo:hi, a:b] for f in fields])  2.5 us
    ppermute x1, starting transfers between devices, on_device(): rest = lax.ppermute(cut(NEAR, FAR, 0, rows), 'grow', down)  1.92 us
    ppermute x1, starting transfers between devices, on_device(): lax.ppermute(cut(0, FAR, rows - HALO, rows), both, diagonal(east))  1.92 us
  transfers between devices with their start and end apart: 6, of which 2 were waited for; matrix products, arithmetic and copies ran while one was open for 1% of the time, Pallas kernels for 24%

profile of v1, /device:TPU:1, one launch (start us, length us, event | category | flops | bytes accessed | tf_op | source)
XLA Modules:
  0.0 58.6 jit_solution(16804145641152622329)
XLA Ops:
  0.6 1.1 %slice_bitcast_fusion.2 = f32[1,7,32,512]{3,2,1,0:T(8,128)S(1)} fusion(f32[16,32,512]{2,1,0:T(8,128)} %refs_0_.1), kind=kLoop, calls=%fused_computation.4 | loop fusion | bytes 917504 | tf_op jit(solution)/shard_map/stack | solution.py:278
  1.7 1.2 %slice_bitcast_fusion = (f32[1,7,32,512]{3,2,1,0:T(8,128)S(1)}, f32[1,7,32,512]{3,2,1,0:T(8,128)S(1)}) fusion(f32[16,32,512]{2,1,0:T(8,128)} %refs_2_.1, f32[16,32,512]{2,1,0:T(8,128)} %refs_1_.1), kind=kLoop, calls=%fused_computation.2 | loop fusion | bytes 1835008 | tf_op jit(solution)/shard_map/stack | solution.py:278
  2.9 0.0 copy-start
  2.9 0.0 copy-start.1
  3.0 0.0 copy-start.2
  3.0 0.1 pad_maximum_fusion
  3.1 5.3 %collective-permute-start.3 = (f32[3,7,32,512]{3,2,1,0:T(8,128)S(1)}, f32[3,7,32,512]{3,2,1,0:T(8,128)S(1)}, u32[]{:S(2)}, u32[]{:S(2)}) collective-permute-start(f32[3,7,32,512]{3,2,1,0:T(8,128)S(1)} %pad_maximum_fusion), channel_id=1, source_target_pairs={{1,0},{2,1},{3,2},{4,3},{5,4},{6,5},{7,6},{8,7},{9,8},{10,9},{11,1... | collective-permute-start | bytes 4128776 | tf_op jit(solution)/shard_map/ppermute | solution.py:284
  8.4 0.0 copy-done
  8.4 0.0 copy-done.1
  8.5 0.0 copy-done.2
  8.5 1.9 %collective-permute-start = (f32[3,3,32,512]{3,2,1,0:T(8,128)S(1)}, f32[3,3,32,512]{3,2,1,0:T(8,128)S(1)}, u32[]{:S(2)}, u32[]{:S(2)}) collective-permute-start(f32[3,3,32,512]{3,2,1,0:T(8,128)S(1)} %pad_maximum_fusion.1), channel_id=1, source_target_pairs={{1,0},{2,1},{3,2},{4,3},{5,4},{6,5},{7,6},{8,7},{9,8},{10,9},{11,1... | collective-permute-start | bytes 1769480 | tf_op jit(solution)/shard_map/ppermute | solution.py:290
  10.5 0.1 slice_bitcast_fusion.8
  10.5 0.1 slice_bitcast_fusion.6
  10.7 0.1 pad_maximum_fusion.4
  10.7 0.1 collective-permute-start.4
  10.8 0.1 pad_maximum_fusion.2
  10.9 1.9 %collective-permute-start.1 = (f32[3,10,2,512]{3,2,1,0:T(2,128)S(1)}, f32[3,10,2,512]{3,2,1,0:T(2,128)S(1)}, u32[]{:S(2)}, u32[]{:S(2)}) collective-permute-start(f32[3,10,2,512]{3,2,1,0:T(2,128)S(1)} %pad_maximum_fusion.2), channel_id=1, source_target_pairs={{1,16},{2,17},{3,18},{4,19},{5,20},{6,21},{7,22},{8,23},{9,24},{10... | collective-permute-start | bytes 368648 | tf_op jit(solution)/shard_map/ppermute | solution.py:288
  12.8 0.1 pad_maximum_fusion.3
  12.9 5.2 %collective-permute-start.2 = (f32[3,10,2,512]{3,2,1,0:T(2,128)S(1)}, f32[3,10,2,512]{3,2,1,0:T(2,128)S(1)}, u32[]{:S(2)}, u32[]{:S(2)}) collective-permute-start(f32[3,10,2,512]{3,2,1,0:T(2,128)S(1)} %pad_maximum_fusion.3), channel_id=1, source_target_pairs={{17,0},{18,1},{19,2},{20,3},{21,4},{22,5},{23,6},{24,7},{25,8},{26... | collective-permute-start | bytes 368648 | tf_op jit(solution)/shard_map/ppermute | solution.py:289
  18.0 0.1 pad_maximum_fusion.5
  18.1 18.3 %collective-permute-done.1 = f32[3,10,2,512]{3,2,1,0:T(2,128)S(1)} collective-permute-done((f32[3,10,2,512]{3,2,1,0:T(2,128)S(1)}, f32[3,10,2,512]{3,2,1,0:T(2,128)S(1)}, u32[]{:S(2)}, u32[]{:S(2)}) %collective-permute-start.1) | collective-permute-done | bytes 122912 | tf_op jit(solution)/shard_map/ppermute | solution.py:288
  36.4 0.5 collective-permute-start.5
  37.0 0.0 collective-permute-done.2
  37.0 0.0 copy-start.3
  37.1 0.0 collective-permute-done.4.refs_3_
  37.1 3.1 %collective-permute-done.5.refs_4_ = f32[3,10,2,512]{3,2,1,0:T(2,128)S(1)} collective-permute-done((f32[3,10,2,512]{3,2,1,0:T(2,128)S(1)}, f32[3,10,2,512]{3,2,1,0:T(2,128)S(1)}, u32[]{:S(2)}, u32[]{:S(2)}) %collective-permute-start.5) | collective-permute-done | bytes 122912 | tf_op jit(solution)/shard_map/ppermute | solution.py:287
  40.2 6.5 %first_run.1 = (f32[16,32,512]{2,1,0:T(8,128)}, f32[16,32,512]{2,1,0:T(8,128)}, f32[16,32,512]{2,1,0:T(8,128)}, f32[2,2,3,40,512]{4,3,2,1,0:T(8,128)S(1)}) custom-call(f32[16,32,512]{2,1,0:T(8,128)S(1)} %copy-done.2, f32[16,32,512]{2,1,0:T(8,128)S(1)} %copy-done.1, f32[16,32,512]{2,1,0:T(8,128)S(1)} %copy-done, ...), custom_call_target="tpu_custom_call" | custom-call | flops 28016640 | bytes 9338880 | tf_op jit(solution)/shard_map/first_run/pallas_call | solution.py:252
  46.7 0.0 collective-permute-done.3.refs_0_
  46.7 0.0 copy-done.3
  46.7 7.5 %next_run.1 = (f32[16,32,512]{2,1,0:T(8,128)}, f32[16,32,512]{2,1,0:T(8,128)}, f32[16,32,512]{2,1,0:T(8,128)}, f32[2,2,3,40,512]{4,3,2,1,0:T(8,128)S(1)}) custom-call(f32[3,7,32,512]{3,2,1,0:T(8,128)S(1)} %collective-permute-done.3.refs_0_, f32[3,7,2,512]{3,2,1,0:T(2,128)S(1)} %slice.90.refs_1_, ...), custom_call_target="tpu_custom_call", output_to_operand_aliasing={{0}: (5, {}), {1}: (6, {}), {2}: (7, {})} | custom-call | flops 28999680 | bytes 9666560 | tf_op jit(solution)/shard_map/next_run/pallas_call | solution.py:252
  54.2 0.0 collective-permute-done.refs_0_
  54.2 4.4 %last_run.1 = (f32[16,32,512]{2,1,0:T(8,128)}, f32[16,32,512]{2,1,0:T(8,128)}, f32[16,32,512]{2,1,0:T(8,128)}) custom-call(f32[3,3,32,512]{3,2,1,0:T(8,128)S(1)} %collective-permute-done.refs_0_, f32[3,3,2,512]{3,2,1,0:T(2,128)S(1)} %slice.88.refs_1_, ...), custom_call_target="tpu_custom_call", output_to_operand_aliasing={{0}: (5, {}), {1}: (6, {}), {2}: (7, {})} | custom-call | flops 15237120 | bytes 5079040 | tf_op jit(solution)/shard_map/last_run/pallas_call | solution.py:252
  (7 shorter events, 0.1 us)
Async XLA Ops:
  2.9 5.5 %copy-start = (f32[16,32,512]{2,1,0:T(8,128)S(1)}, f32[16,32,512]{2,1,0:T(8,128)}, u32[]{:S(2)}) copy-start(f32[16,32,512]{2,1,0:T(8,128)} %refs_2_.1) | copy-start | bytes 3145732
  2.9 5.5 %copy-start.1 = (f32[16,32,512]{2,1,0:T(8,128)S(1)}, f32[16,32,512]{2,1,0:T(8,128)}, u32[]{:S(2)}) copy-start(f32[16,32,512]{2,1,0:T(8,128)} %refs_1_.1) | copy-start | bytes 3145732
  3.0 5.5 %copy-start.2 = (f32[16,32,512]{2,1,0:T(8,128)S(1)}, f32[16,32,512]{2,1,0:T(8,128)}, u32[]{:S(2)}) copy-start(f32[16,32,512]{2,1,0:T(8,128)} %refs_0_.1) | copy-start | bytes 3145732
  3.1 43.6 %collective-permute-start.3 = (f32[3,7,32,512]{3,2,1,0:T(8,128)S(1)}, f32[3,7,32,512]{3,2,1,0:T(8,128)S(1)}, u32[]{:S(2)}, u32[]{:S(2)}) collective-permute-start(f32[3,7,32,512]{3,2,1,0:T(8,128)S(1)} %pad_maximum_fusion), channel_id=1, source_target_pairs={{1,0},{2,1},{3,2},{4,3},{5,4},{6,5},{7,6},{8,7},{9,8},{10,9},{11,1... | collective-permute-start | bytes 4128776 | tf_op jit(solution)/shard_map/ppermute | solution.py:284
  8.5 45.7 %collective-permute-start = (f32[3,3,32,512]{3,2,1,0:T(8,128)S(1)}, f32[3,3,32,512]{3,2,1,0:T(8,128)S(1)}, u32[]{:S(2)}, u32[]{:S(2)}) collective-permute-start(f32[3,3,32,512]{3,2,1,0:T(8,128)S(1)} %pad_maximum_fusion.1), channel_id=1, source_target_pairs={{1,0},{2,1},{3,2},{4,3},{5,4},{6,5},{7,6},{8,7},{9,8},{10,9},{11,1... | collective-permute-start | bytes 1769480 | tf_op jit(solution)/shard_map/ppermute | solution.py:290
  10.7 26.3 %collective-permute-start.4 = (f32[3,10,2,512]{3,2,1,0:T(2,128)S(1)}, f32[3,10,2,512]{3,2,1,0:T(2,128)S(1)}, u32[]{:S(2)}, u32[]{:S(2)}) collective-permute-start(f32[3,10,2,512]{3,2,1,0:T(2,128)S(1)} %pad_maximum_fusion.4), channel_id=1, source_target_pairs={{0,16},{16,32},{32,48},{48,64},{64,80},{80,96},{96,112},{112,128},... | collective-permute-start | bytes 368648 | tf_op jit(solution)/shard_map/ppermute | solution.py:286
  10.9 25.6 %collective-permute-start.1 = (f32[3,10,2,512]{3,2,1,0:T(2,128)S(1)}, f32[3,10,2,512]{3,2,1,0:T(2,128)S(1)}, u32[]{:S(2)}, u32[]{:S(2)}) collective-permute-start(f32[3,10,2,512]{3,2,1,0:T(2,128)S(1)} %pad_maximum_fusion.2), channel_id=1, source_target_pairs={{1,16},{2,17},{3,18},{4,19},{5,20},{6,21},{7,22},{8,23},{9,24},{10... | collective-permute-start | bytes 368648 | tf_op jit(solution)/shard_map/ppermute | solution.py:288
  12.9 24.1 %collective-permute-start.2 = (f32[3,10,2,512]{3,2,1,0:T(2,128)S(1)}, f32[3,10,2,512]{3,2,1,0:T(2,128)S(1)}, u32[]{:S(2)}, u32[]{:S(2)}) collective-permute-start(f32[3,10,2,512]{3,2,1,0:T(2,128)S(1)} %pad_maximum_fusion.3), channel_id=1, source_target_pairs={{17,0},{18,1},{19,2},{20,3},{21,4},{22,5},{23,6},{24,7},{25,8},{26... | collective-permute-start | bytes 368648 | tf_op jit(solution)/shard_map/ppermute | solution.py:289
  36.4 3.7 %collective-permute-start.5 = (f32[3,10,2,512]{3,2,1,0:T(2,128)S(1)}, f32[3,10,2,512]{3,2,1,0:T(2,128)S(1)}, u32[]{:S(2)}, u32[]{:S(2)}) collective-permute-start(f32[3,10,2,512]{3,2,1,0:T(2,128)S(1)} %pad_maximum_fusion.5), channel_id=1, source_target_pairs={{16,0},{32,16},{48,32},{64,48},{80,64},{96,80},{112,96},{128,112},... | collective-permute-start | bytes 368648 | tf_op jit(solution)/shard_map/ppermute | solution.py:287
  37.0 9.7 %copy-start.3 = (f32[8,32,512]{2,1,0:T(8,128)S(1)}, f32[8,32,512]{2,1,0:T(8,128)}, u32[]{:S(2)}) copy-start(f32[8,32,512]{2,1,0:T(8,128)} %refs_4_.3) | copy-start | bytes 1572868

commit v2 on v1

v2 whole, which is shorter than its diff:
```python
import functools

import jax
import jax.numpy as jnp
from jax import lax
from jax.experimental import pallas as pl
from jax.experimental.pallas import tpu as pltpu
from jax.sharding import PartitionSpec as P

STEPS = 2
SHIFT = 8

DT = 0.09
PART = 0.3
DU = 0.5
DP = 0.3
MOB = 0.5
ALPHA = DT * DP / 4.0
MU = DT * MOB / 2.0

HALO = STEPS
ROWS = 32
EXT = ROWS + 8
TILES = EXT // 8
FAR = SHIFT + HALO


def tile(t):
    return pl.ds(8 * t, 8)


def put(base, i, t, s, u, p):
    scaled = ALPHA * p
    carried = p * (MU - MU * p)
    base[i, 0, tile(t)] = s
    base[i, 1, tile(t)] = u
    base[i, 2, tile(t)] = p
    base[i, 3, tile(t)] = scaled + carried
    base[i, 4, tile(t)] = s * (scaled - carried)
    base[i, 5, tile(t)] = s * u


def around(base, i, f, t, sub):
    c = base[i, f, tile(t)]
    before = base[i, f, tile((t - 1) % TILES)]
    after = base[i, f, tile((t + 1) % TILES)]
    n = base[i - 1, f, tile(t)] + base[i + 1, f, tile(t)]
    n = n + pltpu.roll(jnp.where(sub == 7, before, c), 1, 0)
    n = n + pltpu.roll(jnp.where(sub == 0, after, c), 7, 0)
    n = n + pltpu.roll(c, 1, 1)
    n = n + pltpu.roll(c, c.shape[1] - 1, 1)
    return c, n


def advance(base, i, t, sub, theta, gain):
    s, ns = around(base, i, 0, t, sub)
    u, nu = around(base, i, 1, t, sub)
    p = base[i, 2, tile(t)]
    g, ng = around(base, i, 3, t, sub)
    sh, nsh = around(base, i, 4, t, sub)
    su, nsu = around(base, i, 5, t, sub)
    phi = 1.0 - s
    hump = 1.0 - phi * phi
    drive = (u + p) + theta
    rise = ((6.0 * s - ns) + hump * (phi - (hump * drive) * 2.0)) * gain
    flux = (s * nu + nsu) - (u * ns + 6.0 * su)
    weight = PART + (0.5 * (1.0 - PART)) * s
    source = (DT * DU / 4.0) * flux + (0.5 + (0.5 * (1.0 - PART)) * u) * rise
    u_new = u + source * pltpu.reciprocal(weight, full_range=False)
    p_new = p + ((s * ng + nsh) - (g * ns + 6.0 * sh))
    return phi + rise, u_new, p_new


def pack(lo, chunks, *refs):
    fields, held, refs = refs[:4], refs[4:8], refs[8:]
    parts, (east, west, sem) = refs[: len(chunks)], refs[len(chunks) :]
    planes = fields[0].shape[0]
    own, lowest = [], []
    for f in range(3):
        own.append(pltpu.make_async_copy(fields[f].at[pl.ds(lo, planes - lo)], held[f], sem.at[f, 0]))
        first, copies = 0, []
        for k, (part, count) in enumerate(zip(parts, chunks)):
            copies.append(pltpu.make_async_copy(fields[f].at[pl.ds(first, count)], part.at[f], sem.at[f, 1 + k]))
            first += count
        lowest.append(copies)
    entering = pltpu.make_async_copy(fields[3], held[3], sem.at[3, 0])
    for f in range(3):
        for c in [own[f], *lowest[f]]:
            c.start()
    entering.start()
    for f in range(3):
        first = 0
        for part, count, c in zip(parts, chunks, lowest[f]):
            c.wait()

            @pl.loop(0, min(count, lo - first))
            def _(i):
                east[f, first + i] = part[f, i, ROWS - HALO : ROWS]
                west[f, first + i] = part[f, i, 0:HALO]

            first += count
        own[f].wait()

        @pl.loop(0, planes - lo)
        def _(i):
            east[f, lo + i] = held[f][i, ROWS - HALO : ROWS]
            west[f, lo + i] = held[f][i, 0:HALO]

    entering.wait()


def pack_sides(left, right, part, _, mixed, __):
    n, t_all = part.shape[1], ROWS // 8

    @pl.loop(0, n)
    def _(i):
        for f in range(3):
            for t in range(t_all):
                mixed[f, t_all * i + t] = part[f, i, tile(t)]

    @pl.loop(0, FAR // 2)
    def _(i):
        for f in range(3):
            rows = [a[f, i + h] for h in (0, FAR // 2) for a in (right, left)]
            mixed[f, t_all * n + i] = jnp.concatenate(rows, axis=0)


def segment(own, tiled, sides, lo, start, n_new, total, planes, *refs):
    refs = list(refs)
    take = lambda n: [refs.pop(0) for _ in range(n)]
    if own:
        fields = take(3)
        left, right = take(2)
    else:
        inner, mixed, inflow = take(3)
        take(5)
    outs = take(3)
    base0, base1 = take(2)
    res, out_sem = take(2)
    grow = lax.axis_index("grow")
    is_top = grow == lax.axis_size("grow") - 1
    sub = lax.broadcasted_iota(jnp.int32, (8, res.shape[-1]), 0)
    mid0 = start + (1 if own else -1)
    out0 = start + (2 if own else -2)
    n_mid, n_out = (n_new - 2, n_new - 4) if own else (n_new, n_new)
    far0 = start - planes

    @pl.loop(0, n_new)
    def _(i):
        for t in range(ROWS // 8):
            if own:
                phi, u, p = (fields[f][i, tile(t)] for f in range(3))
            elif tiled:
                phi, u, p = (inner[f, ROWS // 8 * i + t] for f in range(3))
            else:
                phi, u, p = (inner[f, i, tile(t)] for f in range(3))
            put(base0, start - lo + i, t, 1.0 - phi, u, p)
        ends = []
        for f in range(3):
            if own:
                low, high = left[f, start + i], right[f, start + i]
                ends.append(jnp.concatenate([high, jnp.zeros((4, high.shape[1]), jnp.float32), low], axis=0))
            else:
                upper = far0 + i >= FAR // 2
                both = mixed[f, sides + jnp.where(upper, far0 + i - FAR // 2, far0 + i)]
                ends.append(jnp.where((sub < 4) != upper, both, pltpu.roll(both, 4, 0)))
        put(base0, start - lo + i, TILES - 1, 1.0 - ends[0], ends[1], ends[2])

    def close(base, first, at, n):
        if first <= at < first + n:

            @pl.when(is_top)
            def _():
                base[at] = base[at - 1]

    close(base0, start - lo, planes - lo, n_new)

    def coefficients(plane):
        height = (grow * planes + plane).astype(jnp.float32)
        theta = (height - 0.5 * total) / total
        lag = jnp.full(sub.shape, 1.0 - (1.0 - PART) * theta, jnp.float32)
        return theta, DT / lag

    @pl.loop(0, n_mid)
    def _(i):
        theta, gain = coefficients(mid0 + i)
        for t in range(TILES):
            phi, u, p = advance(base0, mid0 - lo + i, t, sub, theta, gain)
            put(base1, mid0 - lo - 1 + i, t, 1.0 - phi, u, p)

    close(base1, mid0 - lo - 1, planes - lo - 1, n_mid)

    def write(i):
        return [
            pltpu.make_async_copy(res.at[f, i], outs[f].at[out0 - SHIFT + i], out_sem.at[f, i]) for f in range(3)
        ]

    @pl.loop(0, n_out)
    def _(i):
        theta, gain = coefficients(out0 + i)
        for t in range(ROWS // 8):
            phi, u, p = advance(base1, out0 - lo - 1 + i, t, sub, theta, gain)
            res[0, i, tile(t)] = phi
            res[1, i, tile(t)] = u
            res[2, i, tile(t)] = p
        if not own:

            @pl.when(jnp.logical_and(is_top, out0 + i >= planes))
            def _():
                res[0, i] = jnp.full(res.shape[2:], -1.0, jnp.float32)
                res[1, i] = jnp.full(res.shape[2:], -1.0, jnp.float32)
                res[2, i] = inflow[jnp.maximum(out0 - planes + i, 0)]

        for c in write(i):
            c.start()

    @pl.loop(0, n_out)
    def _(i):
        for c in write(i):
            c.wait()


IN_HBM = pl.BlockSpec(memory_space=pltpu.HBM)
IN_VMEM = pl.BlockSpec(memory_space=pltpu.VMEM)
F32 = jnp.float32


def in_vmem(*shape):
    return pltpu.VMEM(shape, F32)


def near_memory(*arrays):
    return [pltpu.with_memory_space_constraint(a, pltpu.VMEM) for a in arrays]


def run(own, tiled, sides, lo, start, n_new, total, planes, shape, ins, outs=None):
    ny = shape[2]
    n_mid, n_out = (n_new - 2, n_new - 4) if own else (n_new, n_new)
    deep = planes - lo + FAR
    out_shape = [jax.ShapeDtypeStruct(shape, F32)] * 3
    out_shape += [in_vmem(deep, 6, EXT, ny), in_vmem(deep - 2, 6, EXT, ny)]
    scratch = [pltpu.VMEM((3, n_out, ROWS, ny), F32), pltpu.SemaphoreType.DMA((3, n_out))]
    alias = {}
    out_specs = [IN_HBM] * 3 + [IN_VMEM] * 2
    args, in_specs = near_memory(*ins), [IN_VMEM] * len(ins)
    if not own:
        alias = {len(args) + k: k for k in range(5)}
        args += list(outs)
        in_specs += [IN_HBM] * 3 + [IN_VMEM] * 2
    cells = (n_new * 10 + n_mid * EXT + n_out * ROWS) * ny
    return pl.pallas_call(
        functools.partial(segment, own, tiled, sides, lo, start, n_new, total, planes),
        out_shape=out_shape,
        in_specs=in_specs,
        out_specs=out_specs,
        scratch_shapes=scratch,
        input_output_aliases=alias,
        compiler_params=pltpu.CompilerParams(vmem_limit_bytes=8 << 20),
        cost_estimate=pl.CostEstimate(flops=COST_FLOPS * cells, bytes_accessed=COST_BYTES * cells, transcendentals=0),
        name="own_run" if own else f"far_run_{start - planes}",
    )(*args)


PACK_LIMIT = 57 << 20
COST_FLOPS, COST_BYTES = 60, 16
CHUNKS = (6, 2, 2)


def on_device(phase, solute, particle, inflow):
    planes, rows, ny = phase.shape
    n_lat, n_grow = lax.axis_size("lat"), lax.axis_size("grow")
    total = float(n_grow * planes)
    down = [(i + 1, i) for i in range(n_grow - 1)]
    to_east = [(i, (i + 1) % n_lat) for i in range(n_lat)]
    to_west = [((i + 1) % n_lat, i) for i in range(n_lat)]
    lo = planes - SHIFT - HALO
    packed = pl.pallas_call(
        functools.partial(pack, lo, CHUNKS),
        out_shape=[in_vmem(planes - lo, rows, ny)] * 3
        + [in_vmem(*inflow.shape)]
        + [in_vmem(3, n, rows, ny) for n in CHUNKS]
        + [in_vmem(3, planes, HALO, ny)] * 2,
        in_specs=[IN_HBM] * 4,
        out_specs=[IN_VMEM] * (6 + len(CHUNKS)),
        scratch_shapes=[pltpu.SemaphoreType.DMA((4, 1 + len(CHUNKS)))],
        compiler_params=pltpu.CompilerParams(vmem_limit_bytes=PACK_LIMIT),
        name="pack",
    )(phase, solute, particle, inflow)
    fields, inflow, (near, more, rest), (east, west) = packed[:3], packed[3], packed[4:-2], packed[-2:]
    near = lax.ppermute(near, "grow", down)
    left = lax.ppermute(east, "lat", to_east)
    right = lax.ppermute(west, "lat", to_west)
    sides = CHUNKS[1] * (rows // 8)
    mixed, rest = pl.pallas_call(
        pack_sides,
        out_shape=[in_vmem(3, sides + FAR // 2, 8, ny), in_vmem(*rest.shape)],
        in_specs=[IN_VMEM] * 4,
        out_specs=[IN_VMEM] * 2,
        input_output_aliases={3: 1},
        compiler_params=pltpu.CompilerParams(vmem_limit_bytes=1 << 20),
        name="pack_sides",
    )(*near_memory(left, right, more, rest))
    mixed = lax.ppermute(mixed, "grow", down)
    rest = lax.ppermute(rest, "grow", down)

    state = run(True, False, 0, lo, lo, planes - lo, total, planes, phase.shape, (*fields, left, right))
    start = planes
    for n, part in zip(CHUNKS, (near, mixed, rest)):
        tiled = part is mixed
        state = run(False, tiled, sides, lo, start, n, total, planes, phase.shape, (part, mixed, inflow), state)
        start += n
    return tuple(state[:3])


def solution(mesh):
    in_specs = (
        P("grow", "lat", None),
        P("grow", "lat", None),
        P("grow", "lat", None),
        P(None, "lat", None),
    )
    out_specs = (P("grow", "lat", None), P("grow", "lat", None), P("grow", "lat", None))
    return jax.shard_map(
        on_device, mesh=mesh, in_specs=in_specs, out_specs=out_specs, check_vma=False
    )
```

time: 59.2 us -> 38.6 us (0.65)
  waiting for transfers between devices: 21.5 us -> 7.39 us
  local copies, waits for them, and re-layouts: 2.55 us -> 0 us
  Pallas kernels: 18.4 us -> 16.1 us
  starting transfers between devices: 14.9 us -> 14.2 us
    ppermute x6 -> x5, waiting for transfers between devices: 21.5 us -> 7.39 us  [the longest x1 5.14 us: on_device(): left = lax.ppermute(east, 'lat', to_east)]
    another operation x6 -> x0, local copies, waits for them, and re-layouts: 2.5 us -> none  [cut(): return jnp.stack([f[lo:hi, a:b] for f in fields])]
    pallas_call x3 -> x6, Pallas kernels: 18.4 us -> 16.1 us  [the longest x4 13.6 us: run(): pl.pallas_call(functools.partial(segment, own, tiled, sides, lo, start, n...]
    ppermute x6 -> x5, starting transfers between devices: 14.9 us -> 14.2 us  [the longest x1 5.15 us: on_device(): near = lax.ppermute(near, 'grow', down)]
  transfers between devices with their start and end apart: 6 -> 5, of which waited for: 2 -> 2; matrix products, arithmetic and copies ran while one was open for 1% -> 0% of each run, Pallas kernels for 24% -> 31%
where the time goes in v2:
time: 38.6 us; the launch traced here: 38.4 us
  Pallas kernels  16.1 us (42%)
  starting transfers between devices  14.2 us (37%)
  waiting for transfers between devices  7.39 us (19%)
  between operations  0.71 us (2%)
    pallas_call x4, Pallas kernels, run(): pl.pallas_call(functools.partial(segment, own, tiled, sides, lo, start, n...  13.6 us
    ppermute x1, starting transfers between devices, on_device(): near = lax.ppermute(near, 'grow', down)  5.15 us
    ppermute x1, waiting for transfers between devices, on_device(): left = lax.ppermute(east, 'lat', to_east)  5.14 us
    ppermute x1, starting transfers between devices, on_device(): right = lax.ppermute(west, 'lat', to_west)  4.77 us
    pallas_call x1, Pallas kernels, on_device(): pl.pallas_call(functools.partial(pack, lo, CHUNKS), out_shape=[in_vmem(pl...  2.43 us
    ppermute x1, starting transfers between devices, on_device(): mixed = lax.ppermute(mixed, 'grow', down)  2.3 us
    ppermute x1, waiting for transfers between devices, on_device(): mixed = lax.ppermute(mixed, 'grow', down)  2.25 us
    ppermute x1, starting transfers between devices, on_device(): rest = lax.ppermute(rest, 'grow', down)  1.92 us
  transfers between devices with their start and end apart: 5, of which 2 were waited for; matrix products, arithmetic and copies ran while one was open for 0% of the time, Pallas kernels for 31%

profile of v2, /device:TPU:1, one launch (start us, length us, event | category | flops | bytes accessed | tf_op | source)
XLA Modules:
  0.0 38.4 jit_solution(16859731803809160035)
XLA Ops:
  0.6 2.4 %pack.1 = (f32[10,32,512]{2,1,0:T(8,128)S(1)}, f32[10,32,512]{2,1,0:T(8,128)S(1)}, f32[10,32,512]{2,1,0:T(8,128)S(1)}, f32[8,32,512]{2,1,0:T(8,128)S(1)}, f32[3,...) custom-call(f32[16,32,512]{2,1,0:T(8,128)} %refs_0_.1, ...), custom_call_target="tpu_custom_call" | custom-call | tf_op jit(solution)/shard_map/pack/pallas_call | solution.py:277
  3.1 5.1 %collective-permute-start.4 = (f32[3,6,32,512]{3,2,1,0:T(8,128)S(1)}, f32[3,6,32,512]{3,2,1,0:T(8,128)S(1)}, u32[]{:S(2)}, u32[]{:S(2)}) collective-permute-start(f32[3,6,32,512]{3,2,1,0:T(8,128)S(1)} %get-tuple-element.39), channel_id=1, source_target_pairs={{1,0},{2,1},{3,2},{4,3},{5,4},{6,5},{7,6},{8,7},{9,8},{10,9},{11,1... | collective-permute-start | bytes 3538952 | tf_op jit(solution)/shard_map/ppermute | solution.py:290
  8.2 0.1 collective-permute-start
  8.3 4.8 %collective-permute-start.1 = (f32[3,16,2,512]{3,2,1,0:T(2,128)S(1)}, f32[3,16,2,512]{3,2,1,0:T(2,128)S(1)}, u32[]{:S(2)}, u32[]{:S(2)}) collective-permute-start(f32[3,16,2,512]{3,2,1,0:T(2,128)S(1)} %get-tuple-element.33), channel_id=1, source_target_pairs={{16,0},{32,16},{48,32},{64,48},{80,64},{96,80},{112,96},{128,112},... | collective-permute-start | bytes 589832 | tf_op jit(solution)/shard_map/ppermute | solution.py:292
  13.1 5.1 %collective-permute-done.left.refs_3_ = f32[3,16,2,512]{3,2,1,0:T(2,128)S(1)} collective-permute-done((f32[3,16,2,512]{3,2,1,0:T(2,128)S(1)}, f32[3,16,2,512]{3,2,1,0:T(2,128)S(1)}, u32[]{:S(2)}, u32[]{:S(2)}) %collective-permute-start) | collective-permute-done | bytes 196640 | tf_op jit(solution)/shard_map/ppermute | solution.py:291
  18.2 0.0 collective-permute-done.1.right.refs_4_
  18.2 0.1 pack_sides.1
  18.3 2.3 %collective-permute-start.3 = (f32[3,13,8,512]{3,2,1,0:T(8,128)S(1)}, f32[3,13,8,512]{3,2,1,0:T(8,128)S(1)}, u32[]{:S(2)}, u32[]{:S(2)}) collective-permute-start(f32[3,13,8,512]{3,2,1,0:T(8,128)S(1)} %get-tuple-element.37), channel_id=1, source_target_pairs={{1,0},{2,1},{3,2},{4,3},{5,4},{6,5},{7,6},{8,7},{9,8},{10,9},{11,1... | collective-permute-start | bytes 1916936 | tf_op jit(solution)/shard_map/ppermute | solution.py:303
  20.7 1.9 %collective-permute-start.2 = (f32[3,2,32,512]{3,2,1,0:T(8,128)S(1)}, f32[3,2,32,512]{3,2,1,0:T(8,128)S(1)}, u32[]{:S(2)}, u32[]{:S(2)}) collective-permute-start(f32[3,2,32,512]{3,2,1,0:T(8,128)S(1)} %get-tuple-element.36), channel_id=1, source_target_pairs={{1,0},{2,1},{3,2},{4,3},{5,4},{6,5},{7,6},{8,7},{9,8},{10,9},{11,1... | collective-permute-start | bytes 1179656 | tf_op jit(solution)/shard_map/ppermute | solution.py:304
  22.6 5.2 %own_run.1 = (f32[16,32,512]{2,1,0:T(8,128)}, f32[16,32,512]{2,1,0:T(8,128)}, f32[16,32,512]{2,1,0:T(8,128)}, f32[20,6,40,512]{3,2,1,0:T(8,128)S(1)}, f32[18,6,40,512]{3,2,1,0:T(8,128)S(1)}) custom-call(f32[10,32,512]{2,1,0:T(8,128)S(1)} %get-tuple-element.40.refs_0_, f32[10,32,512]{2,1,0:T(8,128)S(1)} %get-tuple-element.41.refs_1_, ...), custom_call_target="tpu_custom_call" | custom-call | flops 18800640 | bytes 5013504 | tf_op jit(solution)/shard_map/own_run/pallas_call | solution.py:251
  27.8 2.2 %collective-permute-done.3.refs_1_.refs_0_ = f32[3,13,8,512]{3,2,1,0:T(8,128)S(1)} collective-permute-done((f32[3,13,8,512]{3,2,1,0:T(8,128)S(1)}, f32[3,13,8,512]{3,2,1,0:T(8,128)S(1)}, u32[]{:S(2)}, u32[]{:S(2)}) %collective-permute-start.3) | collective-permute-done | bytes 639008 | tf_op jit(solution)/shard_map/ppermute | solution.py:303
  30.1 0.0 collective-permute-done.4.refs_0_
  30.1 4.4 %far_run_0.1 = (f32[16,32,512]{2,1,0:T(8,128)}, f32[16,32,512]{2,1,0:T(8,128)}, f32[16,32,512]{2,1,0:T(8,128)}, f32[20,6,40,512]{3,2,1,0:T(8,128)S(1)}, f32[18,6,40,512]{3,2,1,0:T(8,128)S(1)}) custom-call(f32[3,6,32,512]{3,2,1,0:T(8,128)S(1)} %collective-permute-done.4.refs_0_, ...), custom_call_target="tpu_custom_call", output_to_operand_aliasing={{0}: (3, {}), {1}: (4, {}), {2}: (5, {}), {3}: (6, {}), {4}... | custom-call | flops 15114240 | bytes 4030464 | tf_op jit(solution)/shard_map/far_run_0/pallas_call | solution.py:251
  34.5 1.9 %far_run_6.1 = (f32[16,32,512]{2,1,0:T(8,128)}, f32[16,32,512]{2,1,0:T(8,128)}, f32[16,32,512]{2,1,0:T(8,128)}, f32[20,6,40,512]{3,2,1,0:T(8,128)S(1)}, f32[18,6,40,512]{3,2,1,0:T(8,128)S(1)}) custom-call(f32[3,13,8,512]{3,2,1,0:T(8,128)S(1)} %collective-permute-done.3.refs_1_.refs_0_,, ...), custom_call_target="tpu_custom_call", output_to_operand_aliasing={{0}: (3, {}), {1}: (4, {}), {2}: (5, {}), {3}: (6, {}), {4}... | custom-call | flops 5038080 | bytes 1343488 | tf_op jit(solution)/shard_map/far_run_6/pallas_call | solution.py:251
  36.5 0.0 collective-permute-done.2.refs_0_
  36.5 1.9 %far_run_8.1 = (f32[16,32,512]{2,1,0:T(8,128)}, f32[16,32,512]{2,1,0:T(8,128)}, f32[16,32,512]{2,1,0:T(8,128)}, f32[20,6,40,512]{3,2,1,0:T(8,128)S(1)}, f32[18,6,40,512]{3,2,1,0:T(8,128)S(1)}) custom-call(f32[3,2,32,512]{3,2,1,0:T(8,128)S(1)} %collective-permute-done.2.refs_0_, ...), custom_call_target="tpu_custom_call", output_to_operand_aliasing={{0}: (3, {}), {1}: (4, {}), {2}: (5, {}), {3}: (6, {}), {4}... | custom-call | flops 5038080 | bytes 1343488 | tf_op jit(solution)/shard_map/far_run_8/pallas_call | solution.py:251
Async XLA Ops:
  3.1 27.0 %collective-permute-start.4 = (f32[3,6,32,512]{3,2,1,0:T(8,128)S(1)}, f32[3,6,32,512]{3,2,1,0:T(8,128)S(1)}, u32[]{:S(2)}, u32[]{:S(2)}) collective-permute-start(f32[3,6,32,512]{3,2,1,0:T(8,128)S(1)} %get-tuple-element.39), channel_id=1, source_target_pairs={{1,0},{2,1},{3,2},{4,3},{5,4},{6,5},{7,6},{8,7},{9,8},{10,9},{11,1... | collective-permute-start | bytes 3538952 | tf_op jit(solution)/shard_map/ppermute | solution.py:290
  8.2 10.0 %collective-permute-start = (f32[3,16,2,512]{3,2,1,0:T(2,128)S(1)}, f32[3,16,2,512]{3,2,1,0:T(2,128)S(1)}, u32[]{:S(2)}, u32[]{:S(2)}) collective-permute-start(f32[3,16,2,512]{3,2,1,0:T(2,128)S(1)} %get-tuple-element.32), channel_id=1, source_target_pairs={{0,16},{16,32},{32,48},{48,64},{64,80},{80,96},{96,112},{112,128},... | collective-permute-start | bytes 589832 | tf_op jit(solution)/shard_map/ppermute | solution.py:291
  8.3 9.9 %collective-permute-start.1 = (f32[3,16,2,512]{3,2,1,0:T(2,128)S(1)}, f32[3,16,2,512]{3,2,1,0:T(2,128)S(1)}, u32[]{:S(2)}, u32[]{:S(2)}) collective-permute-start(f32[3,16,2,512]{3,2,1,0:T(2,128)S(1)} %get-tuple-element.33), channel_id=1, source_target_pairs={{16,0},{32,16},{48,32},{64,48},{80,64},{96,80},{112,96},{128,112},... | collective-permute-start | bytes 589832 | tf_op jit(solution)/shard_map/ppermute | solution.py:292
  18.3 11.7 %collective-permute-start.3 = (f32[3,13,8,512]{3,2,1,0:T(8,128)S(1)}, f32[3,13,8,512]{3,2,1,0:T(8,128)S(1)}, u32[]{:S(2)}, u32[]{:S(2)}) collective-permute-start(f32[3,13,8,512]{3,2,1,0:T(8,128)S(1)} %get-tuple-element.37), channel_id=1, source_target_pairs={{1,0},{2,1},{3,2},{4,3},{5,4},{6,5},{7,6},{8,7},{9,8},{10,9},{11,1... | collective-permute-start | bytes 1916936 | tf_op jit(solution)/shard_map/ppermute | solution.py:303
  20.7 15.8 %collective-permute-start.2 = (f32[3,2,32,512]{3,2,1,0:T(8,128)S(1)}, f32[3,2,32,512]{3,2,1,0:T(8,128)S(1)}, u32[]{:S(2)}, u32[]{:S(2)}) collective-permute-start(f32[3,2,32,512]{3,2,1,0:T(8,128)S(1)} %get-tuple-element.36), channel_id=1, source_target_pairs={{1,0},{2,1},{3,2},{4,3},{5,4},{6,5},{7,6},{8,7},{9,8},{10,9},{11,1... | collective-permute-start | bytes 1179656 | tf_op jit(solution)/shard_map/ppermute | solution.py:304

commit v3 on v2

v3 whole, which is shorter than its diff:
```python
import functools

import jax
import jax.numpy as jnp
from jax import lax
from jax.experimental import pallas as pl
from jax.experimental.pallas import tpu as pltpu
from jax.sharding import PartitionSpec as P

STEPS = 2
SHIFT = 8

DT = 0.09
PART = 0.3
DU = 0.5
DP = 0.3
MOB = 0.5
ALPHA = DT * DP / 4.0
MU = DT * MOB / 2.0

HALO = STEPS
ROWS = 32
EXT = ROWS + 8
TILES = EXT // 8
FAR = SHIFT + HALO


def tile(t):
    return pl.ds(8 * t, 8)


def put(base, i, t, s, u, p):
    scaled = ALPHA * p
    carried = p * (MU - MU * p)
    base[i, 0, tile(t)] = s
    base[i, 1, tile(t)] = u
    base[i, 2, tile(t)] = p
    base[i, 3, tile(t)] = scaled + carried
    base[i, 4, tile(t)] = s * (scaled - carried)
    base[i, 5, tile(t)] = s * u


def around(base, i, f, t, sub):
    c = base[i, f, tile(t)]
    before = base[i, f, tile((t - 1) % TILES)]
    after = base[i, f, tile((t + 1) % TILES)]
    n = base[i - 1, f, tile(t)] + base[i + 1, f, tile(t)]
    n = n + pltpu.roll(jnp.where(sub == 7, before, c), 1, 0)
    n = n + pltpu.roll(jnp.where(sub == 0, after, c), 7, 0)
    n = n + pltpu.roll(c, 1, 1)
    n = n + pltpu.roll(c, c.shape[1] - 1, 1)
    return c, n


def advance(base, i, t, sub, theta, gain):
    s, ns = around(base, i, 0, t, sub)
    u, nu = around(base, i, 1, t, sub)
    p = base[i, 2, tile(t)]
    g, ng = around(base, i, 3, t, sub)
    sh, nsh = around(base, i, 4, t, sub)
    su, nsu = around(base, i, 5, t, sub)
    phi = 1.0 - s
    hump = 1.0 - phi * phi
    drive = (u + p) + theta
    rise = ((6.0 * s - ns) + hump * (phi - (hump * drive) * 2.0)) * gain
    flux = (s * nu + nsu) - (u * ns + 6.0 * su)
    weight = PART + (0.5 * (1.0 - PART)) * s
    source = (DT * DU / 4.0) * flux + (0.5 + (0.5 * (1.0 - PART)) * u) * rise
    u_new = u + source * pltpu.reciprocal(weight, full_range=False)
    p_new = p + ((s * ng + nsh) - (g * ns + 6.0 * sh))
    return phi + rise, u_new, p_new


def fetch(phase, solute, particle, near, sem):
    copies = [
        pltpu.make_async_copy(a.at[pl.ds(0, near.shape[1])], near.at[f], sem.at[f])
        for f, a in enumerate((phase, solute, particle))
    ]
    for c in copies:
        c.start()
    for c in copies:
        c.wait()


def pack(lo, chunks, *refs):
    fields, near, held, refs = refs[:4], refs[4], refs[5:9], refs[9:]
    later, (east, west, sem) = refs[: len(chunks) - 1], refs[len(chunks) - 1 :]
    planes = fields[0].shape[0]
    own, lowest = [], []
    for f in range(3):
        own.append(pltpu.make_async_copy(fields[f].at[pl.ds(lo, planes - lo)], held[f], sem.at[f, 0]))
        first, copies = chunks[0], []
        for k, (part, count) in enumerate(zip(later, chunks[1:])):
            copies.append(pltpu.make_async_copy(fields[f].at[pl.ds(first, count)], part.at[f], sem.at[f, 1 + k]))
            first += count
        lowest.append(copies)
    entering = pltpu.make_async_copy(fields[3], held[3], sem.at[3, 0])
    for f in range(3):
        for c in [own[f], *lowest[f]]:
            c.start()
    entering.start()

    @pl.loop(0, min(lo, chunks[0]))
    def _(i):
        for f in range(3):
            east[f, i] = near[f, i, ROWS - HALO : ROWS]
            west[f, i] = near[f, i, 0:HALO]

    for f in range(3):
        own[f].wait()

        @pl.loop(0, planes - lo)
        def _(i):
            east[f, lo + i] = held[f][i, ROWS - HALO : ROWS]
            west[f, lo + i] = held[f][i, 0:HALO]

    for f in range(3):
        for c in lowest[f]:
            c.wait()
    entering.wait()


def pack_sides(left, right, part, _, done, mixed, __):
    n, t_all = part.shape[1], ROWS // 8

    @pl.loop(0, n)
    def _(i):
        for f in range(3):
            for t in range(t_all):
                mixed[f, t_all * i + t] = part[f, i, tile(t)]

    @pl.loop(0, FAR // 2)
    def _(i):
        for f in range(3):
            rows = [a[f, i + h] for h in (0, FAR // 2) for a in (right, left)]
            mixed[f, t_all * n + i] = jnp.concatenate(rows, axis=0)


N_TILES = ROWS // 8


def planewise(n, tiles):
    step = min(n, max(1, 8 // tiles))

    def over(body):
        whole = n // step * step

        @pl.loop(0, whole, step=step)
        def _(i):
            for k in range(step):
                body(i + k)

        for i in range(whole, n):
            body(jnp.int32(i))

    return over


FULL, INNER, OUTER = "full", "inner", "outer"
MIDDLE_TILES = {FULL: range(TILES), INNER: range(N_TILES), OUTER: (0, N_TILES - 1, TILES - 1)}
FINAL_TILES = {FULL: range(N_TILES), INNER: range(1, N_TILES - 1), OUTER: (0, N_TILES - 1)}


def segment(kind, own, tiled, writes, beside, lo, start, n_new, total, planes, ins, outs, base0, base1, res, out_sem):
    ins = list(ins)
    take = lambda n: [ins.pop(0) for _ in range(n)]
    rows_in = kind != OUTER
    sides_in = kind != INNER
    if own:
        if rows_in:
            fields = take(3)
        if sides_in:
            left, right = take(2)
    else:
        if rows_in:
            (inner,) = take(1)
        if sides_in:
            (mixed,) = take(1)
        (inflow,) = take(1)
    grow = lax.axis_index("grow")
    is_top = grow == lax.axis_size("grow") - 1
    sub = lax.broadcasted_iota(jnp.int32, (8, res.shape[-1]), 0)
    mid0 = start + (1 if own else -1)
    out0 = start + (2 if own else -2)
    n_mid, n_out = (n_new - 2, n_new - 4) if own else (n_new, n_new)
    far0 = start - planes

    @pl.loop(0, n_new)
    def _(i):
        for t in range(N_TILES) if rows_in else ():
            if own:
                phi, u, p = (fields[f][i, tile(t)] for f in range(3))
            elif tiled:
                phi, u, p = (inner[f, N_TILES * i + t] for f in range(3))
            else:
                phi, u, p = (inner[f, i, tile(t)] for f in range(3))
            put(base0, start - lo + i, t, 1.0 - phi, u, p)
        ends = []
        for f in range(3) if sides_in else ():
            if own:
                low, high = left[f, start + i], right[f, start + i]
                ends.append(jnp.concatenate([high, jnp.zeros((4, high.shape[1]), jnp.float32), low], axis=0))
            else:
                upper = far0 + i >= FAR // 2
                both = mixed[f, beside + jnp.where(upper, far0 + i - FAR // 2, far0 + i)]
                ends.append(jnp.where((sub < 4) != upper, both, pltpu.roll(both, 4, 0)))
        if sides_in:
            put(base0, start - lo + i, TILES - 1, 1.0 - ends[0], ends[1], ends[2])

    def close(base, first, at, n):
        if first <= at < first + n:

            @pl.when(is_top)
            def _():
                base[at] = base[at - 1]

    close(base0, start - lo, planes - lo, n_new)

    def coefficients(plane):
        height = (grow * planes + plane).astype(jnp.float32)
        theta = (height - 0.5 * total) / total
        lag = jnp.full(sub.shape, 1.0 - (1.0 - PART) * theta, jnp.float32)
        return theta, DT / lag

    @planewise(n_mid, len(MIDDLE_TILES[kind]))
    def _(i):
        theta, gain = coefficients(mid0 + i)
        for t in MIDDLE_TILES[kind]:
            phi, u, p = advance(base0, mid0 - lo + i, t, sub, theta, gain)
            put(base1, mid0 - lo - 1 + i, t, 1.0 - phi, u, p)

    close(base1, mid0 - lo - 1, planes - lo - 1, n_mid)

    def write(i):
        at = out0 - SHIFT + i
        return [pltpu.make_async_copy(res.at[f, at], outs[f].at[at], out_sem.at[f, at]) for f in range(3)]

    @planewise(n_out, len(FINAL_TILES[kind]))
    def _(i):
        theta, gain = coefficients(out0 + i)
        at = out0 - SHIFT + i
        for t in FINAL_TILES[kind]:
            phi, u, p = advance(base1, out0 - lo - 1 + i, t, sub, theta, gain)
            res[0, at, tile(t)] = phi
            res[1, at, tile(t)] = u
            res[2, at, tile(t)] = p
        if kind != INNER and not own:

            @pl.when(jnp.logical_and(is_top, out0 + i >= planes))
            def _():
                res[0, at] = jnp.full(res.shape[2:], -1.0, jnp.float32)
                res[1, at] = jnp.full(res.shape[2:], -1.0, jnp.float32)
                res[2, at] = inflow[jnp.maximum(out0 - planes + i, 0)]

        if writes:
            for c in write(i):
                c.start()

    def finish():
        if writes:

            @pl.loop(0, n_out)
            def _(i):
                for c in write(i):
                    c.wait()

    return finish


def several(parts, ready, n_ins, aliased, *refs):
    ins, refs = refs[:n_ins], refs[n_ins + (6 if aliased else 0) :]
    outs, state, sem = refs[:3], refs[3:6], refs[-1]
    if not aliased:
        refs[6][...] = jnp.zeros_like(refs[6])
    copies = []
    if ready:
        first, run_of = ready[0], pl.ds(*ready)
        for f in range(3):
            copies.append(pltpu.make_async_copy(state[2].at[f, run_of], outs[f].at[run_of], sem.at[f, first]))
    for c in copies:
        c.start()
    waits = [part([ins[k] for k in places], outs, *state, sem) for part, places in parts]
    for c in copies:
        c.wait()
    for wait in waits:
        wait()


IN_HBM = pl.BlockSpec(memory_space=pltpu.HBM)
IN_VMEM = pl.BlockSpec(memory_space=pltpu.VMEM)
F32 = jnp.float32


def in_vmem(*shape):
    return pltpu.VMEM(shape, F32)


def near_memory(*arrays):
    return [pltpu.with_memory_space_constraint(a, pltpu.VMEM) for a in arrays]


def run(name, parts, ins, shape, deep, cost, state=None, ready=None):
    planes, rows, ny = shape
    out_shape = [jax.ShapeDtypeStruct(shape, F32)] * 3
    out_shape += [in_vmem(deep, 6, EXT, ny), in_vmem(deep - 2, 6, EXT, ny), in_vmem(3, *shape)]
    args, in_specs, alias = near_memory(*ins), [IN_VMEM] * len(ins), {}
    out_specs = [IN_HBM] * 3 + [IN_VMEM] * 3
    if state is None:
        out_shape.append(in_vmem(8, 128))
        out_specs.append(IN_VMEM)
    else:
        alias = {len(args) + k: k for k in range(6)}
        args += list(state)
        in_specs += [IN_HBM] * 3 + [IN_VMEM] * 3
    return pl.pallas_call(
        functools.partial(several, parts, ready, len(ins), state is not None),
        out_shape=out_shape,
        in_specs=in_specs,
        out_specs=out_specs,
        scratch_shapes=[pltpu.SemaphoreType.DMA((3, planes))],
        input_output_aliases=alias,
        compiler_params=pltpu.CompilerParams(vmem_limit_bytes=4 << 20),
        cost_estimate=pl.CostEstimate(flops=480 * ny * cost, bytes_accessed=128 * ny * cost, transcendentals=0),
        name=name,
    )(*args)


PACK_LIMIT = 57 << 20
CHUNKS = (7, 1, 2)


def on_device(phase, solute, particle, inflow):
    planes, rows, ny = phase.shape
    n_lat, n_grow = lax.axis_size("lat"), lax.axis_size("grow")
    total = float(n_grow * planes)
    down = [(i + 1, i) for i in range(n_grow - 1)]
    to_east = [(i, (i + 1) % n_lat) for i in range(n_lat)]
    to_west = [((i + 1) % n_lat, i) for i in range(n_lat)]
    lo = planes - SHIFT - HALO
    assert CHUNKS[0] >= lo
    fat = pltpu.CompilerParams(vmem_limit_bytes=PACK_LIMIT)
    near = pl.pallas_call(
        fetch,
        out_shape=in_vmem(3, CHUNKS[0], rows, ny),
        in_specs=[IN_HBM] * 3,
        out_specs=IN_VMEM,
        scratch_shapes=[pltpu.SemaphoreType.DMA((3,))],
        compiler_params=fat,
        name="fetch",
    )(phase, solute, particle)
    packed = pl.pallas_call(
        functools.partial(pack, lo, CHUNKS),
        out_shape=[in_vmem(planes - lo, rows, ny)] * 3
        + [in_vmem(*inflow.shape)]
        + [in_vmem(3, n, rows, ny) for n in CHUNKS[1:]]
        + [in_vmem(3, planes, HALO, ny)] * 2,
        in_specs=[IN_HBM] * 4 + [IN_VMEM],
        out_specs=[IN_VMEM] * (5 + len(CHUNKS)),
        scratch_shapes=[pltpu.SemaphoreType.DMA((4, len(CHUNKS)))],
        compiler_params=fat,
        name="pack",
    )(phase, solute, particle, inflow, *near_memory(near))
    fields, inflow, (more, rest), (east, west) = packed[:3], packed[3], packed[4:-2], packed[-2:]
    near = lax.ppermute(near, "grow", down)
    left = lax.ppermute(east, "lat", to_east)
    right = lax.ppermute(west, "lat", to_west)
    beside = CHUNKS[1] * (rows // 8)

    def part(kind, own, tiled, writes, start, n):
        return functools.partial(segment, kind, own, tiled, writes, beside, lo, start, n, total, planes)

    n, start, deep = CHUNKS, planes, planes - lo + FAR
    own = (lo, planes - lo)
    parts = [(part(INNER, True, False, False, *own), (0, 1, 2))]
    *state, done = run("own_inner", parts, fields, phase.shape, deep, 60)
    mixed, rest = pl.pallas_call(
        pack_sides,
        out_shape=[in_vmem(3, beside + FAR // 2, 8, ny), in_vmem(*rest.shape)],
        in_specs=[IN_VMEM] * 5,
        out_specs=[IN_VMEM] * 2,
        input_output_aliases={3: 1},
        compiler_params=pltpu.CompilerParams(vmem_limit_bytes=1 << 20),
        name="pack_sides",
    )(*near_memory(left, right, more, rest, done))
    mixed = lax.ppermute(mixed, "grow", down)
    rest = lax.ppermute(rest, "grow", down)

    parts = [(part(OUTER, True, False, False, *own), (0, 1))]
    state = run("own_outer", parts, (left, right), phase.shape, deep, 50, state)
    parts = [(part(INNER, False, False, False, start, n[0]), (0, 1))]
    n_own = planes - lo - 2 * HALO
    state = run("near_inner", parts, (near, inflow), phase.shape, deep, 60, state, (0, n_own))
    parts = [
        (part(OUTER, False, False, False, start, n[0]), (0, 1)),
        (part(FULL, False, True, False, start + n[0], n[1]), (0, 0, 1)),
    ]
    state = run("near_outer", parts, (mixed, inflow), phase.shape, deep, 60, state)
    parts = [(part(FULL, False, False, True, start + n[0] + n[1], n[2]), (0, 1, 2))]
    state = run("rest", parts, (rest, mixed, inflow), phase.shape, deep, 20, state, (n_own, n[0] + n[1]))
    return tuple(state[:3])


def solution(mesh):
    in_specs = (
        P("grow", "lat", None),
        P("grow", "lat", None),
        P("grow", "lat", None),
        P(None, "lat", None),
    )
    out_specs = (P("grow", "lat", None), P("grow", "lat", None), P("grow", "lat", None))
    return jax.shard_map(
        on_device, mesh=mesh, in_specs=in_specs, out_specs=out_specs, check_vma=False
    )
```

time: 38.6 us -> 35.8 us (0.927)
  waiting for transfers between devices: 7.39 us -> 1.71 us
  Pallas kernels: 16.1 us -> 18.9 us
    ppermute x1, waiting for transfers between devices: 5.14 us -> 1.7 us  [on_device(): left = lax.ppermute(east, 'lat', to_east)]
    pallas_call x5 -> x7, Pallas kernels: 13.7 us -> 17 us  [the longest x5 15.5 us: run(): pl.pallas_call(functools.partial(several, parts, ready, len(ins), state i...]
    ppermute x1, waiting for transfers between devices: 2.25 us -> 0.01 us  [on_device(): mixed = lax.ppermute(mixed, 'grow', down)]
    pallas_call x1, Pallas kernels: 2.43 us -> 1.92 us  [on_device(): pl.pallas_call(functools.partial(pack, lo, CHUNKS), out_shape=[in_vmem(pl...]
  transfers between devices with their start and end apart: 5 -> 5, of which waited for: 2 -> 1; matrix products, arithmetic and copies ran while one was open for 0% -> 0% of each run, Pallas kernels for 31% -> 43%
where the time goes in v3:
time: 35.8 us; the launch traced here: 35.6 us
  Pallas kernels  18.9 us (53%)
  starting transfers between devices  14.2 us (40%)
  waiting for transfers between devices  1.71 us (5%)
  between operations  0.74 us (2%)
    pallas_call x5, Pallas kernels, run(): pl.pallas_call(functools.partial(several, parts, ready, len(ins), state i...  15.5 us
    ppermute x1, starting transfers between devices, on_device(): near = lax.ppermute(near, 'grow', down)  5.15 us
    ppermute x1, starting transfers between devices, on_device(): right = lax.ppermute(west, 'lat', to_west)  4.77 us
    ppermute x1, starting transfers between devices, on_device(): mixed = lax.ppermute(mixed, 'grow', down)  2.3 us
    pallas_call x1, Pallas kernels, on_device(): pl.pallas_call(functools.partial(pack, lo, CHUNKS), out_shape=[in_vmem(pl...  1.92 us
    ppermute x1, starting transfers between devices, on_device(): rest = lax.ppermute(rest, 'grow', down)  1.92 us
    ppermute x1, waiting for transfers between devices, on_device(): left = lax.ppermute(east, 'lat', to_east)  1.7 us
    pallas_call x1, Pallas kernels, on_device(): pl.pallas_call(fetch, out_shape=in_vmem(3, CHUNKS[0], rows, ny), in_specs...  1.32 us
  transfers between devices with their start and end apart: 5, of which 1 were waited for; matrix products, arithmetic and copies ran while one was open for 0% of the time, Pallas kernels for 43%

profile of v3, /device:TPU:1, one launch (start us, length us, event | category | flops | bytes accessed | tf_op | source)
XLA Modules:
  0.0 35.6 jit_solution(13774374638121337079)
XLA Ops:
  0.6 1.3 %fetch.1.refs_4_ = f32[3,7,32,512]{3,2,1,0:T(8,128)S(1)} custom-call(f32[16,32,512]{2,1,0:T(8,128)} %refs_0_.1, f32[16,32,512]{2,1,0:T(8,128)} %refs_1_.1, f32[16,32,512]{2,1,0:T(8,128)} %refs_2_.1), custom_call_target="tpu_custom_call" | custom-call | tf_op jit(solution)/shard_map/fetch/pallas_call | solution.py:342
  2.0 5.1 %collective-permute-start.4 = (f32[3,7,32,512]{3,2,1,0:T(8,128)S(1)}, f32[3,7,32,512]{3,2,1,0:T(8,128)S(1)}, u32[]{:S(2)}, u32[]{:S(2)}) collective-permute-start(f32[3,7,32,512]{3,2,1,0:T(8,128)S(1)} %fetch.1.refs_4_), channel_id=1, source_target_pairs={{1,0},{2,1},{3,2},{4,3},{5,4},{6,5},{7,6},{8,7},{9,8},{10,9},{11,1... | collective-permute-start | bytes 4128776 | tf_op jit(solution)/shard_map/ppermute | solution.py:364
  7.1 1.9 %pack.1 = (f32[10,32,512]{2,1,0:T(8,128)S(1)}, f32[10,32,512]{2,1,0:T(8,128)S(1)}, f32[10,32,512]{2,1,0:T(8,128)S(1)}, f32[8,32,512]{2,1,0:T(8,128)S(1)}, f32[3,...) custom-call(f32[16,32,512]{2,1,0:T(8,128)} %refs_0_.1, ...), custom_call_target="tpu_custom_call" | custom-call | tf_op jit(solution)/shard_map/pack/pallas_call | solution.py:351
  9.0 0.1 collective-permute-start
  9.1 4.8 %collective-permute-start.1 = (f32[3,16,2,512]{3,2,1,0:T(2,128)S(1)}, f32[3,16,2,512]{3,2,1,0:T(2,128)S(1)}, u32[]{:S(2)}, u32[]{:S(2)}) collective-permute-start(f32[3,16,2,512]{3,2,1,0:T(2,128)S(1)} %get-tuple-element.42), channel_id=1, source_target_pairs={{16,0},{32,16},{48,32},{64,48},{80,64},{96,80},{112,96},{128,112},... | collective-permute-start | bytes 589832 | tf_op jit(solution)/shard_map/ppermute | solution.py:366
  13.9 3.4 %own_inner.1 = (f32[16,32,512]{2,1,0:T(8,128)}, f32[16,32,512]{2,1,0:T(8,128)}, f32[16,32,512]{2,1,0:T(8,128)}, f32[20,6,40,512]{3,2,1,0:T(8,128)S(1)}, f32[18,6...) custom-call(f32[10,32,512]{2,1,0:T(8,128)S(1)} %get-tuple-element.45.refs_0_, ...), custom_call_target="tpu_custom_call" | custom-call | flops 14745600 | bytes 3932160 | tf_op jit(solution)/shard_map/own_inner/pallas_call | solution.py:315
  17.4 1.7 %collective-permute-done.left.refs_0_ = f32[3,16,2,512]{3,2,1,0:T(2,128)S(1)} collective-permute-done((f32[3,16,2,512]{3,2,1,0:T(2,128)S(1)}, f32[3,16,2,512]{3,2,1,0:T(2,128)S(1)}, u32[]{:S(2)}, u32[]{:S(2)}) %collective-permute-start) | collective-permute-done | bytes 196640 | tf_op jit(solution)/shard_map/ppermute | solution.py:365
  19.1 0.0 collective-permute-done.1.right.refs_1_
  19.1 0.1 pack_sides.1
  19.2 2.3 %collective-permute-start.3 = (f32[3,9,8,512]{3,2,1,0:T(8,128)S(1)}, f32[3,9,8,512]{3,2,1,0:T(8,128)S(1)}, u32[]{:S(2)}, u32[]{:S(2)}) collective-permute-start(f32[3,9,8,512]{3,2,1,0:T(8,128)S(1)} %get-tuple-element.50), channel_id=1, source_target_pairs={{1,0},{2,1},{3,2},{4,3},{5,4},{6,5},{7,6},{8,7},{9,8},{10,9},{11,1... | collective-permute-start | bytes 1327112 | tf_op jit(solution)/shard_map/ppermute | solution.py:385
  21.5 1.9 %collective-permute-start.2 = (f32[3,2,32,512]{3,2,1,0:T(8,128)S(1)}, f32[3,2,32,512]{3,2,1,0:T(8,128)S(1)}, u32[]{:S(2)}, u32[]{:S(2)}) collective-permute-start(f32[3,2,32,512]{3,2,1,0:T(8,128)S(1)} %get-tuple-element.49), channel_id=1, source_target_pairs={{1,0},{2,1},{3,2},{4,3},{5,4},{6,5},{7,6},{8,7},{9,8},{10,9},{11,1... | collective-permute-start | bytes 1179656 | tf_op jit(solution)/shard_map/ppermute | solution.py:386
  23.4 2.9 %own_outer.1 = (f32[16,32,512]{2,1,0:T(8,128)}, f32[16,32,512]{2,1,0:T(8,128)}, f32[16,32,512]{2,1,0:T(8,128)}, f32[20,6,40,512]{3,2,1,0:T(8,128)S(1)}, f32[18,6...) custom-call(f32[3,16,2,512]{3,2,1,0:T(2,128)S(1)} %collective-permut, ...), custom_call_target="tpu_custom_call", output_to_operand_aliasing={{0}: (2, {}), {1}: (3, {}), {2}: (4, {}), {3}: (5, {}), {4}... | custom-call | flops 12288000 | bytes 3276800 | tf_op jit(solution)/shard_map/own_outer/pallas_call | solution.py:315
  26.3 0.0 collective-permute-done.4.refs_0_
  26.3 3.2 %near_inner.1 = (f32[16,32,512]{2,1,0:T(8,128)}, f32[16,32,512]{2,1,0:T(8,128)}, f32[16,32,512]{2,1,0:T(8,128)}, f32[20,6,40,512]{3,2,1,0:T(8,128)S(1)}, f32[18,...) custom-call(f32[3,7,32,512]{3,2,1,0:T(8,128)S(1)} %collective-permut, ...), custom_call_target="tpu_custom_call", output_to_operand_aliasing={{0}: (2, {}), {1}: (3, {}), {2}: (4, {}), {3}: (5, {}), {4}... | custom-call | flops 14745600 | bytes 3932160 | tf_op jit(solution)/shard_map/near_inner/pallas_call | solution.py:315
  29.5 0.0 collective-permute-done.3.refs_0_.refs_1_
  29.5 3.6 %near_outer.1 = (f32[16,32,512]{2,1,0:T(8,128)}, f32[16,32,512]{2,1,0:T(8,128)}, f32[16,32,512]{2,1,0:T(8,128)}, f32[20,6,40,512]{3,2,1,0:T(8,128)S(1)}, f32[18,...) custom-call(f32[3,9,8,512]{3,2,1,0:T(8,128)S(1)} %collective-permute, ...), custom_call_target="tpu_custom_call", output_to_operand_aliasing={{0}: (2, {}), {1}: (3, {}), {2}: (4, {}), {3}: (5, {}), {4}... | custom-call | flops 14745600 | bytes 3932160 | tf_op jit(solution)/shard_map/near_outer/pallas_call | solution.py:315
  33.1 0.0 collective-permute-done.2.refs_0_
  33.2 2.4 %rest.1 = (f32[16,32,512]{2,1,0:T(8,128)}, f32[16,32,512]{2,1,0:T(8,128)}, f32[16,32,512]{2,1,0:T(8,128)}, f32[20,6,40,512]{3,2,1,0:T(8,128)S(1)}, f32[18,6,40,5...) custom-call(f32[3,2,32,512]{3,2,1,0:T(8,128)S(1)} %collective-permut, ...), custom_call_target="tpu_custom_call", output_to_operand_aliasing={{0}: (3, {}), {1}: (4, {}), {2}: (5, {}), {3}: (6, {}), {4}... | custom-call | flops 4915200 | bytes 1310720 | tf_op jit(solution)/shard_map/rest/pallas_call | solution.py:315
Async XLA Ops:
  2.0 24.3 %collective-permute-start.4 = (f32[3,7,32,512]{3,2,1,0:T(8,128)S(1)}, f32[3,7,32,512]{3,2,1,0:T(8,128)S(1)}, u32[]{:S(2)}, u32[]{:S(2)}) collective-permute-start(f32[3,7,32,512]{3,2,1,0:T(8,128)S(1)} %fetch.1.refs_4_), channel_id=1, source_target_pairs={{1,0},{2,1},{3,2},{4,3},{5,4},{6,5},{7,6},{8,7},{9,8},{10,9},{11,1... | collective-permute-start | bytes 4128776 | tf_op jit(solution)/shard_map/ppermute | solution.py:364
  9.0 10.0 %collective-permute-start = (f32[3,16,2,512]{3,2,1,0:T(2,128)S(1)}, f32[3,16,2,512]{3,2,1,0:T(2,128)S(1)}, u32[]{:S(2)}, u32[]{:S(2)}) collective-permute-start(f32[3,16,2,512]{3,2,1,0:T(2,128)S(1)} %get-tuple-element.41), channel_id=1, source_target_pairs={{0,16},{16,32},{32,48},{48,64},{64,80},{80,96},{96,112},{112,128},... | collective-permute-start | bytes 589832 | tf_op jit(solution)/shard_map/ppermute | solution.py:365
  9.1 9.9 %collective-permute-start.1 = (f32[3,16,2,512]{3,2,1,0:T(2,128)S(1)}, f32[3,16,2,512]{3,2,1,0:T(2,128)S(1)}, u32[]{:S(2)}, u32[]{:S(2)}) collective-permute-start(f32[3,16,2,512]{3,2,1,0:T(2,128)S(1)} %get-tuple-element.42), channel_id=1, source_target_pairs={{16,0},{32,16},{48,32},{64,48},{80,64},{96,80},{112,96},{128,112},... | collective-permute-start | bytes 589832 | tf_op jit(solution)/shard_map/ppermute | solution.py:366
  19.2 10.4 %collective-permute-start.3 = (f32[3,9,8,512]{3,2,1,0:T(8,128)S(1)}, f32[3,9,8,512]{3,2,1,0:T(8,128)S(1)}, u32[]{:S(2)}, u32[]{:S(2)}) collective-permute-start(f32[3,9,8,512]{3,2,1,0:T(8,128)S(1)} %get-tuple-element.50), channel_id=1, source_target_pairs={{1,0},{2,1},{3,2},{4,3},{5,4},{6,5},{7,6},{8,7},{9,8},{10,9},{11,1... | collective-permute-start | bytes 1327112 | tf_op jit(solution)/shard_map/ppermute | solution.py:385
  21.5 11.7 %collective-permute-start.2 = (f32[3,2,32,512]{3,2,1,0:T(8,128)S(1)}, f32[3,2,32,512]{3,2,1,0:T(8,128)S(1)}, u32[]{:S(2)}, u32[]{:S(2)}) collective-permute-start(f32[3,2,32,512]{3,2,1,0:T(8,128)S(1)} %get-tuple-element.49), channel_id=1, source_target_pairs={{1,0},{2,1},{3,2},{4,3},{5,4},{6,5},{7,6},{8,7},{9,8},{10,9},{11,1... | collective-permute-start | bytes 1179656 | tf_op jit(solution)/shard_map/ppermute | solution.py:386

commit v4 on v3

--- a/solution.py
+++ b/solution.py
@@ -17,6 +17,7 @@
 MOB = 0.5
 ALPHA = DT * DP / 4.0
 MU = DT * MOB / 2.0
+HALF = 0.5 * (1.0 - PART)
 
 HALO = STEPS
 ROWS = 32
@@ -30,13 +31,12 @@
 
 
 def put(base, i, t, s, u, p):
-    scaled = ALPHA * p
-    carried = p * (MU - MU * p)
+    m = MU * p
     base[i, 0, tile(t)] = s
     base[i, 1, tile(t)] = u
     base[i, 2, tile(t)] = p
-    base[i, 3, tile(t)] = scaled + carried
-    base[i, 4, tile(t)] = s * (scaled - carried)
+    base[i, 3, tile(t)] = p * ((ALPHA + MU) - m)
+    base[i, 4, tile(t)] = s * (p * ((ALPHA - MU) + m))
     base[i, 5, tile(t)] = s * u
 
 
@@ -47,28 +47,37 @@
     n = base[i - 1, f, tile(t)] + base[i + 1, f, tile(t)]
     n = n + pltpu.roll(jnp.where(sub == 7, before, c), 1, 0)
     n = n + pltpu.roll(jnp.where(sub == 0, after, c), 7, 0)
-    n = n + pltpu.roll(c, 1, 1)
-    n = n + pltpu.roll(c, c.shape[1] - 1, 1)
     return c, n
+
+
+def along(c):
+    return pltpu.roll(c, 1, 1), pltpu.roll(c, c.shape[1] - 1, 1)
 
 
 def advance(base, i, t, sub, theta, gain):
     s, ns = around(base, i, 0, t, sub)
     u, nu = around(base, i, 1, t, sub)
+    _, nsu = around(base, i, 5, t, sub)
+    (s0, s1), (u0, u1) = along(s), along(u)
+    ns = ns + s0 + s1
+    nu = nu + u0 + u1
+    nsu = nsu + s0 * u0 + s1 * u1
     p = base[i, 2, tile(t)]
     g, ng = around(base, i, 3, t, sub)
     sh, nsh = around(base, i, 4, t, sub)
-    su, nsu = around(base, i, 5, t, sub)
+    (g0, g1), (h0, h1) = along(g), along(sh)
+    ng = ng + g0 + g1
+    nsh = nsh + h0 + h1
+    six = 6.0 * s
     phi = 1.0 - s
     hump = 1.0 - phi * phi
     drive = (u + p) + theta
-    rise = ((6.0 * s - ns) + hump * (phi - (hump * drive) * 2.0)) * gain
-    flux = (s * nu + nsu) - (u * ns + 6.0 * su)
-    weight = PART + (0.5 * (1.0 - PART)) * s
-    source = (DT * DU / 4.0) * flux + (0.5 + (0.5 * (1.0 - PART)) * u) * rise
-    u_new = u + source * pltpu.reciprocal(weight, full_range=False)
+    rise = ((six - ns) + hump * (phi - (hump * drive) * 2.0)) * gain
+    flux = (s * nu + nsu) - u * (ns + six)
+    source = (DT * DU / 4.0 / HALF) * flux + (0.5 / HALF + u) * rise
+    u_new = u + source * pltpu.reciprocal(s + PART / HALF, full_range=False)
     p_new = p + ((s * ng + nsh) - (g * ns + 6.0 * sh))
-    return phi + rise, u_new, p_new
+    return phi, rise, s - rise, u_new, p_new
 
 
 def fetch(phase, solute, particle, near, sem):
@@ -226,8 +235,8 @@
     def _(i):
         theta, gain = coefficients(mid0 + i)
         for t in MIDDLE_TILES[kind]:
-            phi, u, p = advance(base0, mid0 - lo + i, t, sub, theta, gain)
-            put(base1, mid0 - lo - 1 + i, t, 1.0 - phi, u, p)
+            _, _, s, u, p = advance(base0, mid0 - lo + i, t, sub, theta, gain)
+            put(base1, mid0 - lo - 1 + i, t, s, u, p)
 
     close(base1, mid0 - lo - 1, planes - lo - 1, n_mid)
 
@@ -240,8 +249,8 @@
         theta, gain = coefficients(out0 + i)
         at = out0 - SHIFT + i
         for t in FINAL_TILES[kind]:
-            phi, u, p = advance(base1, out0 - lo - 1 + i, t, sub, theta, gain)
-            res[0, at, tile(t)] = phi
+            phi, rise, _, u, p = advance(base1, out0 - lo - 1 + i, t, sub, theta, gain)
+            res[0, at, tile(t)] = phi + rise
             res[1, at, tile(t)] = u
             res[2, at, tile(t)] = p
         if kind != INNER and not own:

time: 35.8 us -> 35.5 us (level)
  Pallas kernels: 18.9 us -> 18 us
  waiting for transfers between devices: 1.71 us -> 2.31 us
    pallas_call x5, Pallas kernels: 15.5 us -> 14.6 us  [run(): pl.pallas_call(functools.partial(several, parts, ready, len(ins), state i...]
    ppermute x1, waiting for transfers between devices: 0.01 us -> 0.43 us  [on_device(): rest = lax.ppermute(rest, 'grow', down)]
  transfers between devices with their start and end apart: 5 -> 5, of which waited for: 1 -> 2; matrix products, arithmetic and copies ran while one was open for 0% -> 0% of each run, Pallas kernels for 43% -> 41%
where the time goes in v4:
time: 35.5 us; the launch traced here: 35.2 us
  Pallas kernels  18 us (51%)
  starting transfers between devices  14.2 us (40%)
  waiting for transfers between devices  2.31 us (7%)
  between operations  0.73 us (2%)
    pallas_call x5, Pallas kernels, run(): pl.pallas_call(functools.partial(several, parts, ready, len(ins), state i...  14.6 us
    ppermute x1, starting transfers between devices, on_device(): near = lax.ppermute(near, 'grow', down)  5.15 us
    ppermute x1, starting transfers between devices, on_device(): right = lax.ppermute(west, 'lat', to_west)  4.77 us
    ppermute x1, starting transfers between devices, on_device(): mixed = lax.ppermute(mixed, 'grow', down)  2.3 us
    pallas_call x1, Pallas kernels, on_device(): pl.pallas_call(functools.partial(pack, lo, CHUNKS), out_shape=[in_vmem(pl...  1.92 us
    ppermute x1, starting transfers between devices, on_device(): rest = lax.ppermute(rest, 'grow', down)  1.92 us
    ppermute x1, waiting for transfers between devices, on_device(): left = lax.ppermute(east, 'lat', to_east)  1.87 us
    pallas_call x1, Pallas kernels, on_device(): pl.pallas_call(fetch, out_shape=in_vmem(3, CHUNKS[0], rows, ny), in_specs...  1.32 us
  transfers between devices with their start and end apart: 5, of which 2 were waited for; matrix products, arithmetic and copies ran while one was open for 0% of the time, Pallas kernels for 41%

profile of v4, /device:TPU:1, one launch (start us, length us, event | category | flops | bytes accessed | tf_op | source)
XLA Modules:
  0.0 35.2 jit_solution(10569842541131800276)
XLA Ops:
  0.6 1.3 %fetch.1.refs_4_ = f32[3,7,32,512]{3,2,1,0:T(8,128)S(1)} custom-call(f32[16,32,512]{2,1,0:T(8,128)} %refs_0_.1, f32[16,32,512]{2,1,0:T(8,128)} %refs_1_.1, f32[16,32,512]{2,1,0:T(8,128)} %refs_2_.1), custom_call_target="tpu_custom_call" | custom-call | tf_op jit(solution)/shard_map/fetch/pallas_call | solution.py:351
  2.0 5.1 %collective-permute-start.4 = (f32[3,7,32,512]{3,2,1,0:T(8,128)S(1)}, f32[3,7,32,512]{3,2,1,0:T(8,128)S(1)}, u32[]{:S(2)}, u32[]{:S(2)}) collective-permute-start(f32[3,7,32,512]{3,2,1,0:T(8,128)S(1)} %fetch.1.refs_4_), channel_id=1, source_target_pairs={{1,0},{2,1},{3,2},{4,3},{5,4},{6,5},{7,6},{8,7},{9,8},{10,9},{11,1... | collective-permute-start | bytes 4128776 | tf_op jit(solution)/shard_map/ppermute | solution.py:373
  7.1 1.9 %pack.1 = (f32[10,32,512]{2,1,0:T(8,128)S(1)}, f32[10,32,512]{2,1,0:T(8,128)S(1)}, f32[10,32,512]{2,1,0:T(8,128)S(1)}, f32[8,32,512]{2,1,0:T(8,128)S(1)}, f32[3,...) custom-call(f32[16,32,512]{2,1,0:T(8,128)} %refs_0_.1, ...), custom_call_target="tpu_custom_call" | custom-call | tf_op jit(solution)/shard_map/pack/pallas_call | solution.py:360
  9.0 0.1 collective-permute-start
  9.1 4.8 %collective-permute-start.1 = (f32[3,16,2,512]{3,2,1,0:T(2,128)S(1)}, f32[3,16,2,512]{3,2,1,0:T(2,128)S(1)}, u32[]{:S(2)}, u32[]{:S(2)}) collective-permute-start(f32[3,16,2,512]{3,2,1,0:T(2,128)S(1)} %get-tuple-element.42), channel_id=1, source_target_pairs={{16,0},{32,16},{48,32},{64,48},{80,64},{96,80},{112,96},{128,112},... | collective-permute-start | bytes 589832 | tf_op jit(solution)/shard_map/ppermute | solution.py:375
  13.9 3.3 %own_inner.1 = (f32[16,32,512]{2,1,0:T(8,128)}, f32[16,32,512]{2,1,0:T(8,128)}, f32[16,32,512]{2,1,0:T(8,128)}, f32[20,6,40,512]{3,2,1,0:T(8,128)S(1)}, f32[18,6...) custom-call(f32[10,32,512]{2,1,0:T(8,128)S(1)} %get-tuple-element.45.refs_0_, ...), custom_call_target="tpu_custom_call" | custom-call | flops 14745600 | bytes 3932160 | tf_op jit(solution)/shard_map/own_inner/pallas_call | solution.py:324
  17.2 1.9 %collective-permute-done.left.refs_0_ = f32[3,16,2,512]{3,2,1,0:T(2,128)S(1)} collective-permute-done((f32[3,16,2,512]{3,2,1,0:T(2,128)S(1)}, f32[3,16,2,512]{3,2,1,0:T(2,128)S(1)}, u32[]{:S(2)}, u32[]{:S(2)}) %collective-permute-start) | collective-permute-done | bytes 196640 | tf_op jit(solution)/shard_map/ppermute | solution.py:374
  19.1 0.0 collective-permute-done.1.right.refs_1_
  19.1 0.1 pack_sides.1
  19.2 2.3 %collective-permute-start.3 = (f32[3,9,8,512]{3,2,1,0:T(8,128)S(1)}, f32[3,9,8,512]{3,2,1,0:T(8,128)S(1)}, u32[]{:S(2)}, u32[]{:S(2)}) collective-permute-start(f32[3,9,8,512]{3,2,1,0:T(8,128)S(1)} %get-tuple-element.50), channel_id=1, source_target_pairs={{1,0},{2,1},{3,2},{4,3},{5,4},{6,5},{7,6},{8,7},{9,8},{10,9},{11,1... | collective-permute-start | bytes 1327112 | tf_op jit(solution)/shard_map/ppermute | solution.py:394
  21.5 1.9 %collective-permute-start.2 = (f32[3,2,32,512]{3,2,1,0:T(8,128)S(1)}, f32[3,2,32,512]{3,2,1,0:T(8,128)S(1)}, u32[]{:S(2)}, u32[]{:S(2)}) collective-permute-start(f32[3,2,32,512]{3,2,1,0:T(8,128)S(1)} %get-tuple-element.49), channel_id=1, source_target_pairs={{1,0},{2,1},{3,2},{4,3},{5,4},{6,5},{7,6},{8,7},{9,8},{10,9},{11,1... | collective-permute-start | bytes 1179656 | tf_op jit(solution)/shard_map/ppermute | solution.py:395
  23.4 2.7 %own_outer.1 = (f32[16,32,512]{2,1,0:T(8,128)}, f32[16,32,512]{2,1,0:T(8,128)}, f32[16,32,512]{2,1,0:T(8,128)}, f32[20,6,40,512]{3,2,1,0:T(8,128)S(1)}, f32[18,6...) custom-call(f32[3,16,2,512]{3,2,1,0:T(2,128)S(1)} %collective-permut, ...), custom_call_target="tpu_custom_call", output_to_operand_aliasing={{0}: (2, {}), {1}: (3, {}), {2}: (4, {}), {3}: (5, {}), {4}... | custom-call | flops 12288000 | bytes 3276800 | tf_op jit(solution)/shard_map/own_outer/pallas_call | solution.py:324
  26.1 0.0 collective-permute-done.4.refs_0_
  26.1 3.1 %near_inner.1 = (f32[16,32,512]{2,1,0:T(8,128)}, f32[16,32,512]{2,1,0:T(8,128)}, f32[16,32,512]{2,1,0:T(8,128)}, f32[20,6,40,512]{3,2,1,0:T(8,128)S(1)}, f32[18,...) custom-call(f32[3,7,32,512]{3,2,1,0:T(8,128)S(1)} %collective-permut, ...), custom_call_target="tpu_custom_call", output_to_operand_aliasing={{0}: (2, {}), {1}: (3, {}), {2}: (4, {}), {3}: (5, {}), {4}... | custom-call | flops 14745600 | bytes 3932160 | tf_op jit(solution)/shard_map/near_inner/pallas_call | solution.py:324
  29.2 0.0 collective-permute-done.3.refs_0_.refs_1_
  29.2 3.3 %near_outer.1 = (f32[16,32,512]{2,1,0:T(8,128)}, f32[16,32,512]{2,1,0:T(8,128)}, f32[16,32,512]{2,1,0:T(8,128)}, f32[20,6,40,512]{3,2,1,0:T(8,128)S(1)}, f32[18,...) custom-call(f32[3,9,8,512]{3,2,1,0:T(8,128)S(1)} %collective-permute, ...), custom_call_target="tpu_custom_call", output_to_operand_aliasing={{0}: (2, {}), {1}: (3, {}), {2}: (4, {}), {3}: (5, {}), {4}... | custom-call | flops 14745600 | bytes 3932160 | tf_op jit(solution)/shard_map/near_outer/pallas_call | solution.py:324
  32.6 0.4 %collective-permute-done.2.refs_0_ = f32[3,2,32,512]{3,2,1,0:T(8,128)S(1)} collective-permute-done((f32[3,2,32,512]{3,2,1,0:T(8,128)S(1)}, f32[3,2,32,512]{3,2,1,0:T(8,128)S(1)}, u32[]{:S(2)}, u32[]{:S(2)}) %collective-permute-start.2) | collective-permute-done | bytes 393248 | tf_op jit(solution)/shard_map/ppermute | solution.py:395
  33.0 2.2 %rest.1 = (f32[16,32,512]{2,1,0:T(8,128)}, f32[16,32,512]{2,1,0:T(8,128)}, f32[16,32,512]{2,1,0:T(8,128)}, f32[20,6,40,512]{3,2,1,0:T(8,128)S(1)}, f32[18,6,40,5...) custom-call(f32[3,2,32,512]{3,2,1,0:T(8,128)S(1)} %collective-permut, ...), custom_call_target="tpu_custom_call", output_to_operand_aliasing={{0}: (3, {}), {1}: (4, {}), {2}: (5, {}), {3}: (6, {}), {4}... | custom-call | flops 4915200 | bytes 1310720 | tf_op jit(solution)/shard_map/rest/pallas_call | solution.py:324
Async XLA Ops:
  2.0 24.2 %collective-permute-start.4 = (f32[3,7,32,512]{3,2,1,0:T(8,128)S(1)}, f32[3,7,32,512]{3,2,1,0:T(8,128)S(1)}, u32[]{:S(2)}, u32[]{:S(2)}) collective-permute-start(f32[3,7,32,512]{3,2,1,0:T(8,128)S(1)} %fetch.1.refs_4_), channel_id=1, source_target_pairs={{1,0},{2,1},{3,2},{4,3},{5,4},{6,5},{7,6},{8,7},{9,8},{10,9},{11,1... | collective-permute-start | bytes 4128776 | tf_op jit(solution)/shard_map/ppermute | solution.py:373
  9.0 10.0 %collective-permute-start = (f32[3,16,2,512]{3,2,1,0:T(2,128)S(1)}, f32[3,16,2,512]{3,2,1,0:T(2,128)S(1)}, u32[]{:S(2)}, u32[]{:S(2)}) collective-permute-start(f32[3,16,2,512]{3,2,1,0:T(2,128)S(1)} %get-tuple-element.41), channel_id=1, source_target_pairs={{0,16},{16,32},{32,48},{48,64},{64,80},{80,96},{96,112},{112,128},... | collective-permute-start | bytes 589832 | tf_op jit(solution)/shard_map/ppermute | solution.py:374
  9.1 9.9 %collective-permute-start.1 = (f32[3,16,2,512]{3,2,1,0:T(2,128)S(1)}, f32[3,16,2,512]{3,2,1,0:T(2,128)S(1)}, u32[]{:S(2)}, u32[]{:S(2)}) collective-permute-start(f32[3,16,2,512]{3,2,1,0:T(2,128)S(1)} %get-tuple-element.42), channel_id=1, source_target_pairs={{16,0},{32,16},{48,32},{64,48},{80,64},{96,80},{112,96},{128,112},... | collective-permute-start | bytes 589832 | tf_op jit(solution)/shard_map/ppermute | solution.py:375
  19.2 10.1 %collective-permute-start.3 = (f32[3,9,8,512]{3,2,1,0:T(8,128)S(1)}, f32[3,9,8,512]{3,2,1,0:T(8,128)S(1)}, u32[]{:S(2)}, u32[]{:S(2)}) collective-permute-start(f32[3,9,8,512]{3,2,1,0:T(8,128)S(1)} %get-tuple-element.50), channel_id=1, source_target_pairs={{1,0},{2,1},{3,2},{4,3},{5,4},{6,5},{7,6},{8,7},{9,8},{10,9},{11,1... | collective-permute-start | bytes 1327112 | tf_op jit(solution)/shard_map/ppermute | solution.py:394
  21.5 11.5 %collective-permute-start.2 = (f32[3,2,32,512]{3,2,1,0:T(8,128)S(1)}, f32[3,2,32,512]{3,2,1,0:T(8,128)S(1)}, u32[]{:S(2)}, u32[]{:S(2)}) collective-permute-start(f32[3,2,32,512]{3,2,1,0:T(8,128)S(1)} %get-tuple-element.49), channel_id=1, source_target_pairs={{1,0},{2,1},{3,2},{4,3},{5,4},{6,5},{7,6},{8,7},{9,8},{10,9},{11,1... | collective-permute-start | bytes 1179656 | tf_op jit(solution)/shard_map/ppermute | solution.py:395

commit v5 on v4

--- a/solution.py
+++ b/solution.py
@@ -149,7 +149,7 @@
 
 
 def planewise(n, tiles):
-    step = min(n, max(1, 8 // tiles))
+    step = min(n, max(1, 10 // tiles))
 
     def over(body):
         whole = n // step * step

time: 35.5 us -> 35.4 us (level)
  no operation moved by 1% of the time
where the time goes in v5:
time: 35.4 us; the launch traced here: 35.2 us
  Pallas kernels  17.9 us (51%)
  starting transfers between devices  14.2 us (40%)
  waiting for transfers between devices  2.4 us (7%)
  between operations  0.73 us (2%)
    pallas_call x5, Pallas kernels, run(): pl.pallas_call(functools.partial(several, parts, ready, len(ins), state i...  14.5 us
    ppermute x1, starting transfers between devices, on_device(): near = lax.ppermute(near, 'grow', down)  5.15 us
    ppermute x1, starting transfers between devices, on_device(): right = lax.ppermute(west, 'lat', to_west)  4.77 us
    ppermute x1, starting transfers between devices, on_device(): mixed = lax.ppermute(mixed, 'grow', down)  2.3 us
    pallas_call x1, Pallas kernels, on_device(): pl.pallas_call(functools.partial(pack, lo, CHUNKS), out_shape=[in_vmem(pl...  1.92 us
    ppermute x1, starting transfers between devices, on_device(): rest = lax.ppermute(rest, 'grow', down)  1.92 us
    ppermute x1, waiting for transfers between devices, on_device(): left = lax.ppermute(east, 'lat', to_east)  1.87 us
    pallas_call x1, Pallas kernels, on_device(): pl.pallas_call(fetch, out_shape=in_vmem(3, CHUNKS[0], rows, ny), in_specs...  1.32 us
  transfers between devices with their start and end apart: 5, of which 2 were waited for; matrix products, arithmetic and copies ran while one was open for 0% of the time, Pallas kernels for 41%

profile of v5, /device:TPU:1, one launch (start us, length us, event | category | flops | bytes accessed | tf_op | source)
XLA Modules:
  0.0 35.2 jit_solution(8084022940905098631)
XLA Ops:
  0.6 1.3 %fetch.1.refs_4_ = f32[3,7,32,512]{3,2,1,0:T(8,128)S(1)} custom-call(f32[16,32,512]{2,1,0:T(8,128)} %refs_0_.1, f32[16,32,512]{2,1,0:T(8,128)} %refs_1_.1, f32[16,32,512]{2,1,0:T(8,128)} %refs_2_.1), custom_call_target="tpu_custom_call" | custom-call | tf_op jit(solution)/shard_map/fetch/pallas_call | solution.py:351
  2.0 5.1 %collective-permute-start.4 = (f32[3,7,32,512]{3,2,1,0:T(8,128)S(1)}, f32[3,7,32,512]{3,2,1,0:T(8,128)S(1)}, u32[]{:S(2)}, u32[]{:S(2)}) collective-permute-start(f32[3,7,32,512]{3,2,1,0:T(8,128)S(1)} %fetch.1.refs_4_), channel_id=1, source_target_pairs={{1,0},{2,1},{3,2},{4,3},{5,4},{6,5},{7,6},{8,7},{9,8},{10,9},{11,1... | collective-permute-start | bytes 4128776 | tf_op jit(solution)/shard_map/ppermute | solution.py:373
  7.1 1.9 %pack.1 = (f32[10,32,512]{2,1,0:T(8,128)S(1)}, f32[10,32,512]{2,1,0:T(8,128)S(1)}, f32[10,32,512]{2,1,0:T(8,128)S(1)}, f32[8,32,512]{2,1,0:T(8,128)S(1)}, f32[3,...) custom-call(f32[16,32,512]{2,1,0:T(8,128)} %refs_0_.1, ...), custom_call_target="tpu_custom_call" | custom-call | tf_op jit(solution)/shard_map/pack/pallas_call | solution.py:360
  9.0 0.1 collective-permute-start
  9.1 4.8 %collective-permute-start.1 = (f32[3,16,2,512]{3,2,1,0:T(2,128)S(1)}, f32[3,16,2,512]{3,2,1,0:T(2,128)S(1)}, u32[]{:S(2)}, u32[]{:S(2)}) collective-permute-start(f32[3,16,2,512]{3,2,1,0:T(2,128)S(1)} %get-tuple-element.42), channel_id=1, source_target_pairs={{16,0},{32,16},{48,32},{64,48},{80,64},{96,80},{112,96},{128,112},... | collective-permute-start | bytes 589832 | tf_op jit(solution)/shard_map/ppermute | solution.py:375
  13.9 3.3 %own_inner.1 = (f32[16,32,512]{2,1,0:T(8,128)}, f32[16,32,512]{2,1,0:T(8,128)}, f32[16,32,512]{2,1,0:T(8,128)}, f32[20,6,40,512]{3,2,1,0:T(8,128)S(1)}, f32[18,6...) custom-call(f32[10,32,512]{2,1,0:T(8,128)S(1)} %get-tuple-element.45.refs_0_, ...), custom_call_target="tpu_custom_call" | custom-call | flops 14745600 | bytes 3932160 | tf_op jit(solution)/shard_map/own_inner/pallas_call | solution.py:324
  17.2 1.9 %collective-permute-done.left.refs_0_ = f32[3,16,2,512]{3,2,1,0:T(2,128)S(1)} collective-permute-done((f32[3,16,2,512]{3,2,1,0:T(2,128)S(1)}, f32[3,16,2,512]{3,2,1,0:T(2,128)S(1)}, u32[]{:S(2)}, u32[]{:S(2)}) %collective-permute-start) | collective-permute-done | bytes 196640 | tf_op jit(solution)/shard_map/ppermute | solution.py:374
  19.1 0.0 collective-permute-done.1.right.refs_1_
  19.1 0.1 pack_sides.1
  19.2 2.3 %collective-permute-start.3 = (f32[3,9,8,512]{3,2,1,0:T(8,128)S(1)}, f32[3,9,8,512]{3,2,1,0:T(8,128)S(1)}, u32[]{:S(2)}, u32[]{:S(2)}) collective-permute-start(f32[3,9,8,512]{3,2,1,0:T(8,128)S(1)} %get-tuple-element.50), channel_id=1, source_target_pairs={{1,0},{2,1},{3,2},{4,3},{5,4},{6,5},{7,6},{8,7},{9,8},{10,9},{11,1... | collective-permute-start | bytes 1327112 | tf_op jit(solution)/shard_map/ppermute | solution.py:394
  21.5 1.9 %collective-permute-start.2 = (f32[3,2,32,512]{3,2,1,0:T(8,128)S(1)}, f32[3,2,32,512]{3,2,1,0:T(8,128)S(1)}, u32[]{:S(2)}, u32[]{:S(2)}) collective-permute-start(f32[3,2,32,512]{3,2,1,0:T(8,128)S(1)} %get-tuple-element.49), channel_id=1, source_target_pairs={{1,0},{2,1},{3,2},{4,3},{5,4},{6,5},{7,6},{8,7},{9,8},{10,9},{11,1... | collective-permute-start | bytes 1179656 | tf_op jit(solution)/shard_map/ppermute | solution.py:395
  23.4 2.7 %own_outer.1 = (f32[16,32,512]{2,1,0:T(8,128)}, f32[16,32,512]{2,1,0:T(8,128)}, f32[16,32,512]{2,1,0:T(8,128)}, f32[20,6,40,512]{3,2,1,0:T(8,128)S(1)}, f32[18,6...) custom-call(f32[3,16,2,512]{3,2,1,0:T(2,128)S(1)} %collective-permut, ...), custom_call_target="tpu_custom_call", output_to_operand_aliasing={{0}: (2, {}), {1}: (3, {}), {2}: (4, {}), {3}: (5, {}), {4}... | custom-call | flops 12288000 | bytes 3276800 | tf_op jit(solution)/shard_map/own_outer/pallas_call | solution.py:324
  26.1 0.0 collective-permute-done.4.refs_0_
  26.1 3.1 %near_inner.1 = (f32[16,32,512]{2,1,0:T(8,128)}, f32[16,32,512]{2,1,0:T(8,128)}, f32[16,32,512]{2,1,0:T(8,128)}, f32[20,6,40,512]{3,2,1,0:T(8,128)S(1)}, f32[18,...) custom-call(f32[3,7,32,512]{3,2,1,0:T(8,128)S(1)} %collective-permut, ...), custom_call_target="tpu_custom_call", output_to_operand_aliasing={{0}: (2, {}), {1}: (3, {}), {2}: (4, {}), {3}: (5, {}), {4}... | custom-call | flops 14745600 | bytes 3932160 | tf_op jit(solution)/shard_map/near_inner/pallas_call | solution.py:324
  29.2 0.0 collective-permute-done.3.refs_0_.refs_1_
  29.2 3.3 %near_outer.1 = (f32[16,32,512]{2,1,0:T(8,128)}, f32[16,32,512]{2,1,0:T(8,128)}, f32[16,32,512]{2,1,0:T(8,128)}, f32[20,6,40,512]{3,2,1,0:T(8,128)S(1)}, f32[18,...) custom-call(f32[3,9,8,512]{3,2,1,0:T(8,128)S(1)} %collective-permute, ...), custom_call_target="tpu_custom_call", output_to_operand_aliasing={{0}: (2, {}), {1}: (3, {}), {2}: (4, {}), {3}: (5, {}), {4}... | custom-call | flops 14745600 | bytes 3932160 | tf_op jit(solution)/shard_map/near_outer/pallas_call | solution.py:324
  32.5 0.5 %collective-permute-done.2.refs_0_ = f32[3,2,32,512]{3,2,1,0:T(8,128)S(1)} collective-permute-done((f32[3,2,32,512]{3,2,1,0:T(8,128)S(1)}, f32[3,2,32,512]{3,2,1,0:T(8,128)S(1)}, u32[]{:S(2)}, u32[]{:S(2)}) %collective-permute-start.2) | collective-permute-done | bytes 393248 | tf_op jit(solution)/shard_map/ppermute | solution.py:395
  33.0 2.2 %rest.1 = (f32[16,32,512]{2,1,0:T(8,128)}, f32[16,32,512]{2,1,0:T(8,128)}, f32[16,32,512]{2,1,0:T(8,128)}, f32[20,6,40,512]{3,2,1,0:T(8,128)S(1)}, f32[18,6,40,5...) custom-call(f32[3,2,32,512]{3,2,1,0:T(8,128)S(1)} %collective-permut, ...), custom_call_target="tpu_custom_call", output_to_operand_aliasing={{0}: (3, {}), {1}: (4, {}), {2}: (5, {}), {3}: (6, {}), {4}... | custom-call | flops 4915200 | bytes 1310720 | tf_op jit(solution)/shard_map/rest/pallas_call | solution.py:324
Async XLA Ops:
  2.0 24.1 %collective-permute-start.4 = (f32[3,7,32,512]{3,2,1,0:T(8,128)S(1)}, f32[3,7,32,512]{3,2,1,0:T(8,128)S(1)}, u32[]{:S(2)}, u32[]{:S(2)}) collective-permute-start(f32[3,7,32,512]{3,2,1,0:T(8,128)S(1)} %fetch.1.refs_4_), channel_id=1, source_target_pairs={{1,0},{2,1},{3,2},{4,3},{5,4},{6,5},{7,6},{8,7},{9,8},{10,9},{11,1... | collective-permute-start | bytes 4128776 | tf_op jit(solution)/shard_map/ppermute | solution.py:373
  9.0 10.0 %collective-permute-start = (f32[3,16,2,512]{3,2,1,0:T(2,128)S(1)}, f32[3,16,2,512]{3,2,1,0:T(2,128)S(1)}, u32[]{:S(2)}, u32[]{:S(2)}) collective-permute-start(f32[3,16,2,512]{3,2,1,0:T(2,128)S(1)} %get-tuple-element.41), channel_id=1, source_target_pairs={{0,16},{16,32},{32,48},{48,64},{64,80},{80,96},{96,112},{112,128},... | collective-permute-start | bytes 589832 | tf_op jit(solution)/shard_map/ppermute | solution.py:374
  9.1 9.9 %collective-permute-start.1 = (f32[3,16,2,512]{3,2,1,0:T(2,128)S(1)}, f32[3,16,2,512]{3,2,1,0:T(2,128)S(1)}, u32[]{:S(2)}, u32[]{:S(2)}) collective-permute-start(f32[3,16,2,512]{3,2,1,0:T(2,128)S(1)} %get-tuple-element.42), channel_id=1, source_target_pairs={{16,0},{32,16},{48,32},{64,48},{80,64},{96,80},{112,96},{128,112},... | collective-permute-start | bytes 589832 | tf_op jit(solution)/shard_map/ppermute | solution.py:375
  19.2 10.0 %collective-permute-start.3 = (f32[3,9,8,512]{3,2,1,0:T(8,128)S(1)}, f32[3,9,8,512]{3,2,1,0:T(8,128)S(1)}, u32[]{:S(2)}, u32[]{:S(2)}) collective-permute-start(f32[3,9,8,512]{3,2,1,0:T(8,128)S(1)} %get-tuple-element.50), channel_id=1, source_target_pairs={{1,0},{2,1},{3,2},{4,3},{5,4},{6,5},{7,6},{8,7},{9,8},{10,9},{11,1... | collective-permute-start | bytes 1327112 | tf_op jit(solution)/shard_map/ppermute | solution.py:394
  21.5 11.5 %collective-permute-start.2 = (f32[3,2,32,512]{3,2,1,0:T(8,128)S(1)}, f32[3,2,32,512]{3,2,1,0:T(8,128)S(1)}, u32[]{:S(2)}, u32[]{:S(2)}) collective-permute-start(f32[3,2,32,512]{3,2,1,0:T(8,128)S(1)} %get-tuple-element.49), channel_id=1, source_target_pairs={{1,0},{2,1},{3,2},{4,3},{5,4},{6,5},{7,6},{8,7},{9,8},{10,9},{11,1... | collective-permute-start | bytes 1179656 | tf_op jit(solution)/shard_map/ppermute | solution.py:395
